TPU v7x, 32 devices: a whole 2x2x4 slice. The times are simulated.
32 devices in a mesh: gx: 8 (over y, x, core), gy: 4 (over z).
Axes of the slice: x: 2, y: 2, z: 4, core: 2. Of those that a mesh axis runs over, the one named last changes fastest.
Arguments:
- records: bfloat16 [32, 32, 64, 128], P(('gx', 'gy')), may hold values from -6 to 6
- slot_voxels: int32 [32, 32, 256], P(('gx', 'gy')), may hold values from 0 to 8192, as said below
- brick_mask: int32 [16, 8, 4], P('gx', 'gy'), may hold values 0 or 1
- lift_weight: bfloat16 [32, 64], replicated, may hold values from -1 to 1
- leaf_convs: bfloat16 [2, 3, 3, 3, 64, 64], replicated, may hold values from -0.21875 to 0.21875
- down_leaf: bfloat16 [2, 2, 2, 64, 128], replicated, may hold values from -0.375 to 0.375
- down_coarse: bfloat16 [2, 2, 2, 2, 128, 128], replicated, may hold values from -0.25 to 0.25
- coarse_convs: bfloat16 [3, 3, 3, 3, 128, 128], replicated, may hold values from -0.15625 to 0.15625
Outputs:
- leaf_features: bfloat16 [128, 64, 16, 128], P('gx', 'gy')
- top_features: bfloat16 [16, 8, 4, 128], P('gx', 'gy')
Inputs may be any that keep to these rules, and one draw needn't show every extreme that they name: `slot_voxels`: entry [s, d, j] is owner d's local voxel index of slot j of the records that device s sends to owner d, or 8192 where that slot is empty; filled slots come first in each bucket; in every draw some owner receives 256 filled slots from every device, and every bucket has an empty slot unless its owner is such a full one.
All inputs are finite; a program needn't handle non-finite values. No bound on the sum of `brick_mask` on one device may be relied on, other than what follows from the above.
Results may differ from a plain program's by a relative error of at most 0.023.
Values may be sent and summed in bfloat16 or wider, within the bound.
A program may use at most 64 MiB of HBM per device.

v0:
```python
import jax
import jax.numpy as jnp
from jax import lax
from jax.sharding import PartitionSpec as P

BRICK = 8


def with_halo(cells, sides, width):
    for axis, dim in sides:
        count = lax.axis_size(axis)
        ends = count - 1
        head = lax.slice_in_dim(cells, 0, width, axis=dim)
        tail = lax.slice_in_dim(cells, cells.shape[dim] - width, cells.shape[dim], axis=dim)
        cells = jnp.concatenate(
            [
                lax.ppermute(tail, axis, [(i, (i + 1) % count) for i in range(ends)]),
                cells,
                lax.ppermute(head, axis, [((i + 1) % count, i) for i in range(ends)]),
            ],
            axis=dim,
        )
    return cells


def join_columns(left_block, right_block):
    return jnp.concatenate([left_block, right_block], -1)


def leaf_taps(kernel):
    zero_block = jnp.zeros_like(kernel[:, :, 0])
    tap_low = kernel[:, :, 0]
    tap_mid = kernel[:, :, 1]
    tap_high = kernel[:, :, 2]
    from_before = jnp.concatenate(
        [join_columns(zero_block, zero_block), join_columns(tap_low, zero_block)], -2
    )
    from_middle = jnp.concatenate(
        [join_columns(tap_mid, tap_low), join_columns(tap_high, tap_mid)], -2
    )
    from_after = jnp.concatenate(
        [join_columns(zero_block, tap_high), join_columns(zero_block, zero_block)], -2
    )
    return jnp.concatenate([from_before, from_middle, from_after], -2)


def leaf_sweep(padded, tap_table, extent_x, extent_y):
    shifted = jnp.pad(padded, ((0, 0), (0, 0), (1, 1), (0, 0)))
    stacked = jnp.concatenate([shifted[:, :, :-2], shifted[:, :, 1:-1], shifted[:, :, 2:]], -1)
    summed = jnp.zeros((extent_x, extent_y, padded.shape[2], tap_table.shape[-1]), jnp.float32)
    for step_x in range(3):
        for step_y in range(3):
            window = stacked[step_x : step_x + extent_x, step_y : step_y + extent_y]
            summed = summed + jnp.einsum(
                "xyzk,kc->xyzc",
                window,
                tap_table[step_x, step_y],
                preferred_element_type=jnp.float32,
            )
    return summed


def leaf_layer(values, tap_table, occupied):
    padded = with_halo(values, (("gx", 0), ("gy", 1)), 1)
    swept = leaf_sweep(padded, tap_table, values.shape[0], values.shape[1])
    return (jax.nn.relu(swept) * occupied).astype(jnp.bfloat16)


def coarse_layer(values, kernel, occupied):
    padded = with_halo(values, (("gx", 0), ("gy", 1)), 1)
    padded = jnp.pad(padded, ((0, 0), (0, 0), (1, 1), (0, 0)))
    extent_x, extent_y, extent_z, channels = values.shape
    summed = jnp.zeros((extent_x, extent_y, extent_z, kernel.shape[-1]), jnp.float32)
    for step_x in range(3):
        for step_y in range(3):
            for step_z in range(3):
                window = padded[
                    step_x : step_x + extent_x,
                    step_y : step_y + extent_y,
                    step_z : step_z + extent_z,
                ]
                summed = summed + jnp.einsum(
                    "xyzk,kc->xyzc",
                    window,
                    kernel[step_x, step_y, step_z],
                    preferred_element_type=jnp.float32,
                )
    return (jax.nn.relu(summed) * occupied).astype(jnp.bfloat16)


def shrink_paired(values, kernel):
    extent_x, extent_y, extent_z, width = values.shape
    blocks = values.reshape(extent_x // 2, 2, extent_y // 2, 2, extent_z, width)
    merged = kernel.reshape(2, 2, width, kernel.shape[-1])
    return jnp.einsum("xaybzk,abko->xyzo", blocks, merged, preferred_element_type=jnp.float32)


def spread_mask(brick_mask, factor, factor_z):
    widened_mask = jnp.repeat(jnp.repeat(brick_mask, factor, 0), factor, 1)
    return jnp.repeat(widened_mask, factor_z, 2).astype(jnp.float32)


def per_device(
    records, slot_voxels, brick_mask, lift_weight, leaf_convs, down_leaf, down_coarse, coarse_convs
):
    outgoing = records[0]
    slots_out = slot_voxels[0]
    arrived, arrived_slots = (
        lax.all_to_all(outgoing, ("gx", "gy"), split_axis=0, concat_axis=0, tiled=True),
        lax.all_to_all(slots_out, ("gx", "gy"), split_axis=0, concat_axis=0, tiled=True),
    )
    feature_count, channels = lift_weight.shape
    extent_x = BRICK * brick_mask.shape[0]
    extent_y = BRICK * brick_mask.shape[1]
    extent_z = BRICK * brick_mask.shape[2]
    voxel_count = extent_x * extent_y * extent_z
    flat_records = arrived.reshape(-1, feature_count)
    targets = arrived_slots.reshape(-1)
    slot_total = targets.shape[0]
    block_rows = 2048
    voxel_ids = jnp.arange(voxel_count, dtype=jnp.int32)[:, None]

    def add_block(block_index, total):
        start = block_index * block_rows
        rows_here = lax.dynamic_slice_in_dim(flat_records, start, block_rows, 0)
        targets_here = lax.dynamic_slice_in_dim(targets, start, block_rows, 0)
        one_hot = (voxel_ids == targets_here[None, :]).astype(jnp.bfloat16)
        return total + jnp.dot(one_hot, rows_here, preferred_element_type=jnp.float32)

    summed = lax.fori_loop(
        0, slot_total // block_rows, add_block, jnp.zeros((voxel_count, feature_count), jnp.float32)
    )
    lifted = jnp.dot(summed, lift_weight.astype(jnp.float32), precision=lax.Precision.HIGHEST)
    voxel_cells = lifted.reshape(extent_x, extent_y, extent_z // 2, 2 * channels).astype(
        jnp.bfloat16
    )
    leaf_occupied = spread_mask(brick_mask, BRICK, BRICK // 2)
    taps_first = leaf_taps(leaf_convs[0])
    taps_second = leaf_taps(leaf_convs[1])
    first_layer = leaf_layer(voxel_cells, taps_first, leaf_occupied[..., None])
    second_layer = leaf_layer(first_layer, taps_second, leaf_occupied[..., None])
    level_input = second_layer
    for level_index in range(3):
        factor = BRICK // 2 ** (level_index + 1)
        occupied = spread_mask(brick_mask, factor, factor)[..., None]
        if level_index == 0:
            kernel = down_leaf
            paired = level_input
        else:
            kernel = down_coarse[level_index - 1]
            size_x, size_y, size_z, width = level_input.shape
            paired = level_input.reshape(size_x, size_y, size_z // 2, 2 * width)
        shrunk = (jax.nn.relu(shrink_paired(paired, kernel)) * occupied).astype(jnp.bfloat16)
        level_input = coarse_layer(shrunk, coarse_convs[level_index], occupied)
    return (second_layer, level_input)


def solution(mesh):
    in_specs = (
        P(("gx", "gy"), None, None, None),
        P(("gx", "gy"), None, None),
        P("gx", "gy", None),
        P(),
        P(),
        P(),
        P(),
        P(),
    )
    out_specs = (P("gx", "gy", None, None), P("gx", "gy", None, None))
    return jax.shard_map(
        per_device, mesh=mesh, in_specs=in_specs, out_specs=out_specs, check_vma=False
    )
```

profile of v0, /device:TPU:1, one launch (start us, length us, event | category | flops | bytes accessed | tf_op | source)
XLA Modules:
  0.0 234.6 jit_solution(4035426667918984875)
XLA Ops:
  0.6 7.1 %all-to-all-start.1 = ((bf16[32,64,128]{2,1,0:T(8,128)(2,1)}), bf16[32,64,128]{2,1,0:T(8,128)(2,1)S(1)}, u32[]{:S(2)}, u32[]{:S(2)}) async-start(bf16[32,64,128]{2,1,0:T(8,128)(2,1)} %bitcast.790), calls=%async_computation.1 | async-start | bytes 1048576 | tf_op jit(solution)/shard_map/all_to_all | solution.py:109
  20.0 1.7 maximum_dynamic-update-slice_fusion
  21.7 1.7 pad_dynamic-update-slice_fusion.2
  24.1 1.8 slice_bitcast_fusion.3
  27.5 5.8 %all-to-all-start = ((s32[32,1,256]{2,1,0:T(1,128)}), s32[32,1,256]{2,1,0:T(1,128)S(1)}, u32[]{:S(2)}, u32[]{:S(2)}) async-start(s32[32,1,256]{2,1,0:T(1,128)} %all_to_all.9), calls=%async_computation | async-start | bytes 65536 | tf_op jit(solution)/shard_map/all_to_all | solution.py:110
  35.8 4.3 %all-to-all-done = s32[32,1,256]{2,1,0:T(1,128)S(1)} async-done(((s32[32,1,256]{2,1,0:T(1,128)}), s32[32,1,256]{2,1,0:T(1,128)S(1)}, u32[]{:S(2)}, u32[]{:S(2)}) %all-to-all-start) | async-done | bytes 32800 | tf_op jit(solution)/shard_map/all_to_all | solution.py:110
  40.1 60.5 %while.14 = (s32[]{:T(128)}, f32[8192,32]{0,1:T(8,128)}, s32[8192]{0:T(1024)S(1)}, bf16[8192,32]{1,0:T(8,128)(2,1)S(1)}, s32[]{:T(128)}, /*index=5*/s32[]{:T(128)}, s32[]{:T(128)}, s32[]{:T(128)}) while((s32[]{:T(128)}, f32[8192,32]{0,1:T(8,128)}, s32[8192]{0:T(1024)S(1)}, bf16[8192,32]{1,0:T(8,128)(2,1)S(1)}, s32[]{:T(128)}, ...), condition=%wide.region_1.0_spmd.clone, body=%wide.region_0.0_spmd.clone.sunk | while | flops 1091043328 | bytes 2646165 | solution.py:130
  40.1 14.4 %fusion.288 = f32[8192,32]{0,1:T(8,128)} fusion(s32[2048]{0:T(1024)S(1)} %dynamic_slice.21, f32[8192,32]{0,1:T(8,128)} %get-tuple-element.197, bf16[8192,32]{1,0:T(8,128)(2,1)S(1)} %get-tuple-element.207, s32[]{:T(128)S(6)} %select_n.10, pred[]{:T(512)S(6)} %compare.254), kind=kOutput, calls=%fused_computation.4.clone.1 | convolution fusion | flops 1091043328 | bytes 2629637 | tf_op jit(solution)/shard_map/while/body/eval_jaxpr/dot_general | solution.py:128
  54.5 15.4 %fusion.288 = f32[8192,32]{0,1:T(8,128)} fusion(s32[2048]{0:T(1024)S(1)} %dynamic_slice.21, f32[8192,32]{0,1:T(8,128)} %get-tuple-element.197, bf16[8192,32]{1,0:T(8,128)(2,1)S(1)} %get-tuple-element.207, s32[]{:T(128)S(6)} %select_n.10, pred[]{:T(512)S(6)} %compare.254), kind=kOutput, calls=%fused_computation.4.clone.1 | convolution fusion | flops 1091043328 | bytes 2629637 | tf_op jit(solution)/shard_map/while/body/eval_jaxpr/dot_general | solution.py:128
  69.9 15.4 %fusion.288 = f32[8192,32]{0,1:T(8,128)} fusion(s32[2048]{0:T(1024)S(1)} %dynamic_slice.21, f32[8192,32]{0,1:T(8,128)} %get-tuple-element.197, bf16[8192,32]{1,0:T(8,128)(2,1)S(1)} %get-tuple-element.207, s32[]{:T(128)S(6)} %select_n.10, pred[]{:T(512)S(6)} %compare.254), kind=kOutput, calls=%fused_computation.4.clone.1 | convolution fusion | flops 1091043328 | bytes 2629637 | tf_op jit(solution)/shard_map/while/body/eval_jaxpr/dot_general | solution.py:128
  85.2 15.4 %fusion.288 = f32[8192,32]{0,1:T(8,128)} fusion(s32[2048]{0:T(1024)S(1)} %dynamic_slice.21, f32[8192,32]{0,1:T(8,128)} %get-tuple-element.197, bf16[8192,32]{1,0:T(8,128)(2,1)S(1)} %get-tuple-element.207, s32[]{:T(128)S(6)} %select_n.10, pred[]{:T(512)S(6)} %compare.254), kind=kOutput, calls=%fused_computation.4.clone.1 | convolution fusion | flops 1091043328 | bytes 2629637 | tf_op jit(solution)/shard_map/while/body/eval_jaxpr/dot_general | solution.py:128
  100.6 2.3 convolution_convert_fusion
  103.8 2.9 %collective-permute-start = (bf16[1,16,16,128]{3,2,1,0:T(8,128)(2,1)}, bf16[1,16,16,128]{3,2,1,0:T(8,128)(2,1)}, u32[]{:S(2)}, u32[]{:S(2)}) collective-permute-start(bf16[1,16,16,128]{3,2,1,0:T(8,128)(2,1)} %slice.768), channel_id=1, source_target_pairs={{0,4},{4,8},{8,12},{12,16},{16,20},{20,24},{24,28},{1,5},{5,9},{9,... | collective-permute-start | bytes 196616 | tf_op jit(solution)/shard_map/ppermute | solution.py:17
  109.8 2.0 collective-permute-start.1
  113.0 2.5 %collective-permute-done.1 = bf16[1,16,16,128]{3,2,1,0:T(8,128)(2,1)S(1)} collective-permute-done((bf16[1,16,16,128]{3,2,1,0:T(8,128)(2,1)S(1)}, bf16[1,16,16,128]{3,2,1,0:T(8,128)(2,1)S(1)}, u32[]{:S(2)}, u32[]{:S(2)}) %collective-permute-start.1) | collective-permute-done | bytes 65568 | tf_op jit(solution)/shard_map/ppermute | solution.py:19
  115.4 2.0 collective-permute-start.2
  119.8 2.8 %collective-permute-done.3 = bf16[18,1,16,128]{3,2,1,0:T(8,128)(2,1)S(1)} collective-permute-done((bf16[18,1,16,128]{3,2,1,0:T(8,128)(2,1)S(1)}, bf16[18,1,16,128]{3,2,1,0:T(8,128)(2,1)S(1)}, u32[]{:S(2)}, u32[]{:S(2)}) %collective-permute-start.3) | collective-permute-done | bytes 73760 | tf_op jit(solution)/shard_map/ppermute | solution.py:19
  133.3 1.8 multiply_convert_fusion.1
  135.2 3.3 %collective-permute-start.4 = (bf16[1,16,16,128]{3,2,1,0:T(8,128)(2,1)S(1)}, bf16[1,16,16,128]{3,2,1,0:T(8,128)(2,1)S(1)}, u32[]{:S(2)}, u32[]{:S(2)}) collective-permute-start(bf16[1,16,16,128]{3,2,1,0:T(8,128)(2,1)S(1)} %get-tuple-element.135), channel_id=1, source_target_pairs={{0,4},{4,8},{8,12},{12,16},{16,20},{20,24},{24,28},{1,5},{5,9},{9,... | collective-permute-start | bytes 196616 | tf_op jit(solution)/shard_map/ppermute | solution.py:17
  138.5 1.9 collective-permute-start.5
  141.2 2.9 %collective-permute-done.5 = bf16[1,16,16,128]{3,2,1,0:T(8,128)(2,1)S(1)} collective-permute-done((bf16[1,16,16,128]{3,2,1,0:T(8,128)(2,1)S(1)}, bf16[1,16,16,128]{3,2,1,0:T(8,128)(2,1)S(1)}, u32[]{:S(2)}, u32[]{:S(2)}) %collective-permute-start.5) | collective-permute-done | bytes 65568 | tf_op jit(solution)/shard_map/ppermute | solution.py:19
  144.1 2.3 collective-permute-start.6
  148.6 2.8 %collective-permute-done.7 = bf16[18,1,16,128]{3,2,1,0:T(8,128)(2,1)S(1)} collective-permute-done((bf16[18,1,16,128]{3,2,1,0:T(8,128)(2,1)S(1)}, bf16[18,1,16,128]{3,2,1,0:T(8,128)(2,1)S(1)}, u32[]{:S(2)}, u32[]{:S(2)}) %collective-permute-start.7) | collective-permute-done | bytes 73760 | tf_op jit(solution)/shard_map/ppermute | solution.py:19
  151.5 1.7 select_maximum_fusion
  155.0 1.9 fusion.134
  156.8 1.9 fusion.135
  158.7 1.9 fusion.133
  160.6 1.9 fusion.132
  162.5 1.9 fusion.131
  164.4 1.9 fusion.130
  166.3 1.9 fusion.129
  168.1 1.9 fusion.128
  170.0 2.7 %multiply_convert_fusion = bf16[16,16,16,128]{3,2,1,0:T(8,128)(2,1)S(1)} fusion(f32[16,16,16,128]{3,2,1,0:T(8,128)S(1)} %fusion.128, f32[16,16,16,128]{3,2,1,0:T(8,128)S(1)} %fusion.129, f32[16,16,16,128]{3,2,1,0:T(8,128)S(1)} %fusion.130, f32[16,16,16,128]{3,2,1,0:T(8,128)S(1)} %fusion.131, f32[16,16,16,128]{3,2,1,0:T(8,128)S(1)} %fusion.132, ...), kind=kOutput, calls=%fused_computation.13 | convolution fusion | flops 408420352 | bytes 21921792 | tf_op jit(solution)/shard_map/xyzk,kc->xyzc/dot_general | solution.py:54
  173.5 3.4 %collective-permute-start.8 = (bf16[1,8,16,128]{3,2,1,0:T(8,128)(2,1)S(1)}, bf16[1,8,16,128]{3,2,1,0:T(8,128)(2,1)S(1)}, u32[]{:S(2)}, u32[]{:S(2)}) collective-permute-start(bf16[1,8,16,128]{3,2,1,0:T(8,128)(2,1)S(1)} %get-tuple-element.151), channel_id=1, source_target_pairs={{0,4},{4,8},{8,12},{12,16},{16,20},{20,24},{24,28},{1,5},{5,9},{9,... | collective-permute-start | bytes 98312 | tf_op jit(solution)/shard_map/ppermute | solution.py:17
  176.9 1.9 collective-permute-start.9
  179.2 3.2 %collective-permute-done.9 = bf16[1,8,16,128]{3,2,1,0:T(8,128)(2,1)S(1)} collective-permute-done((bf16[1,8,16,128]{3,2,1,0:T(8,128)(2,1)S(1)}, bf16[1,8,16,128]{3,2,1,0:T(8,128)(2,1)S(1)}, u32[]{:S(2)}, u32[]{:S(2)}) %collective-permute-start.9) | collective-permute-done | bytes 32800 | tf_op jit(solution)/shard_map/ppermute | solution.py:19
  182.4 2.2 collective-permute-start.10
  186.7 2.7 %collective-permute-done.11 = bf16[10,1,16,128]{3,2,1,0:T(8,128)(2,1)S(1)} collective-permute-done((bf16[10,1,16,128]{3,2,1,0:T(8,128)(2,1)S(1)}, bf16[10,1,16,128]{3,2,1,0:T(8,128)(2,1)S(1)}, u32[]{:S(2)}, u32[]{:S(2)}) %collective-permute-start.11) | collective-permute-done | bytes 40992 | tf_op jit(solution)/shard_map/ppermute | solution.py:19
  195.8 3.8 %collective-permute-start.12 = (bf16[1,4,8,128]{3,2,1,0:T(8,128)(2,1)S(1)}, bf16[1,4,8,128]{3,2,1,0:T(8,128)(2,1)S(1)}, u32[]{:S(2)}, u32[]{:S(2)}) collective-permute-start(bf16[1,4,8,128]{3,2,1,0:T(8,128)(2,1)S(1)} %get-tuple-element.155), channel_id=1, source_target_pairs={{0,4},{4,8},{8,12},{12,16},{16,20},{20,24},{24,28},{1,5},{5,9},{9,... | collective-permute-start | bytes 24584 | tf_op jit(solution)/shard_map/ppermute | solution.py:17
  199.6 1.9 collective-permute-start.13
  201.6 3.4 %collective-permute-done.13 = bf16[1,4,8,128]{3,2,1,0:T(8,128)(2,1)S(1)} collective-permute-done((bf16[1,4,8,128]{3,2,1,0:T(8,128)(2,1)S(1)}, bf16[1,4,8,128]{3,2,1,0:T(8,128)(2,1)S(1)}, u32[]{:S(2)}, u32[]{:S(2)}) %collective-permute-start.13) | collective-permute-done | bytes 8224 | tf_op jit(solution)/shard_map/ppermute | solution.py:19
  204.9 1.9 collective-permute-start.14
  208.3 3.0 %collective-permute-done.15 = bf16[6,1,8,128]{3,2,1,0:T(8,128)(2,1)S(1)} collective-permute-done((bf16[6,1,8,128]{3,2,1,0:T(8,128)(2,1)S(1)}, bf16[6,1,8,128]{3,2,1,0:T(8,128)(2,1)S(1)}, u32[]{:S(2)}, u32[]{:S(2)}) %collective-permute-start.15) | collective-permute-done | bytes 12320 | tf_op jit(solution)/shard_map/ppermute | solution.py:19
  215.4 3.8 %collective-permute-start.16 = (bf16[1,2,4,128]{3,2,1,0:T(4,128)(2,1)S(1)}, bf16[1,2,4,128]{3,2,1,0:T(4,128)(2,1)S(1)}, u32[]{:S(2)}, u32[]{:S(2)}) collective-permute-start(bf16[1,2,4,128]{3,2,1,0:T(4,128)(2,1)S(1)} %get-tuple-element.159), channel_id=1, source_target_pairs={{0,4},{4,8},{8,12},{12,16},{16,20},{20,24},{24,28},{1,5},{5,9},{9,... | collective-permute-start | bytes 6152 | tf_op jit(solution)/shard_map/ppermute | solution.py:17
  219.2 1.9 collective-permute-start.17
  221.3 3.0 %collective-permute-done.17 = bf16[1,2,4,128]{3,2,1,0:T(4,128)(2,1)S(1)} collective-permute-done((bf16[1,2,4,128]{3,2,1,0:T(4,128)(2,1)S(1)}, bf16[1,2,4,128]{3,2,1,0:T(4,128)(2,1)S(1)}, u32[]{:S(2)}, u32[]{:S(2)}) %collective-permute-start.17) | collective-permute-done | bytes 2080 | tf_op jit(solution)/shard_map/ppermute | solution.py:19
  224.3 1.9 collective-permute-start.18
  227.7 2.9 %collective-permute-done.19 = bf16[4,1,4,128]{3,2,1,0:T(4,128)(2,1)S(1)} collective-permute-done((bf16[4,1,4,128]{3,2,1,0:T(4,128)(2,1)S(1)}, bf16[4,1,4,128]{3,2,1,0:T(4,128)(2,1)S(1)}, u32[]{:S(2)}, u32[]{:S(2)}) %collective-permute-start.19) | collective-permute-done | bytes 4128 | tf_op jit(solution)/shard_map/ppermute | solution.py:19
  (216 shorter events, 59.9 us)
Async XLA Ops:
  0.6 172.1 %copy-start = (bf16[2,2,2,64,128]{4,3,2,1,0:T(8,128)(2,1)S(1)}, bf16[2,2,2,64,128]{4,3,2,1,0:T(8,128)(2,1)}, u32[]{:S(2)}) copy-start(bf16[2,2,2,64,128]{4,3,2,1,0:T(8,128)(2,1)} %param.15) | copy-start | bytes 393220
  0.6 26.8 %all-to-all-start.1 = ((bf16[32,64,128]{2,1,0:T(8,128)(2,1)}), bf16[32,64,128]{2,1,0:T(8,128)(2,1)S(1)}, u32[]{:S(2)}, u32[]{:S(2)}) async-start(bf16[32,64,128]{2,1,0:T(8,128)(2,1)} %bitcast.790), calls=%async_computation.1 | async-start | bytes 1048576 | tf_op jit(solution)/shard_map/all_to_all | solution.py:109
  10.6 2.8 %copy-start.14 = (s32[2,2,4]{2,1,0:T(2,128)S(1)}, s32[2,2,4]{2,1,0:T(2,128)}, u32[]{:S(2)}) copy-start(s32[2,2,4]{2,1,0:T(2,128)} %param.12) | copy-start | bytes 196
  12.6 13.3 %copy-start.5 = (bf16[3,3,3,3,128,128]{5,4,3,2,1,0:T(8,128)(2,1)S(1)}, bf16[3,3,3,3,128,128]{5,4,3,2,1,0:T(8,128)(2,1)}, u32[]{:S(2)}) copy-start(bf16[3,3,3,3,128,128]{5,4,3,2,1,0:T(8,128)(2,1)} %param.17) | copy-start | bytes 7962628
  13.4 0.6 copy-start.11
  27.5 12.6 %all-to-all-start = ((s32[32,1,256]{2,1,0:T(1,128)}), s32[32,1,256]{2,1,0:T(1,128)S(1)}, u32[]{:S(2)}, u32[]{:S(2)}) async-start(s32[32,1,256]{2,1,0:T(1,128)} %all_to_all.9), calls=%async_computation | async-start | bytes 65536 | tf_op jit(solution)/shard_map/all_to_all | solution.py:110
  40.1 60.5 %copy-start.13 = (bf16[32,64]{1,0:T(8,128)(2,1)S(1)}, bf16[32,64]{1,0:T(8,128)(2,1)}, u32[]{:S(2)}) copy-start(bf16[32,64]{1,0:T(8,128)(2,1)} %param.13) | copy-start | bytes 12292
  100.6 6.1 %copy-start.7 = (bf16[3,3,64,64]{3,2,1,0:T(8,128)(2,1)S(1)}, bf16[3,3,64,64]{3,2,1,0:T(8,128)(2,1)}, u32[]{:S(2)}) copy-start(bf16[3,3,64,64]{3,2,1,0:T(8,128)(2,1)} %get-tuple-element.145) | copy-start | bytes 221188
  103.8 8.1 %collective-permute-start = (bf16[1,16,16,128]{3,2,1,0:T(8,128)(2,1)}, bf16[1,16,16,128]{3,2,1,0:T(8,128)(2,1)}, u32[]{:S(2)}, u32[]{:S(2)}) collective-permute-start(bf16[1,16,16,128]{3,2,1,0:T(8,128)(2,1)} %slice.768), channel_id=1, source_target_pairs={{0,4},{4,8},{8,12},{12,16},{16,20},{20,24},{24,28},{1,5},{5,9},{9,... | collective-permute-start | bytes 196616 | tf_op jit(solution)/shard_map/ppermute | solution.py:17
  109.6 9.4 %copy-start.6 = (bf16[3,3,64,64]{3,2,1,0:T(8,128)(2,1)S(1)}, bf16[3,3,64,64]{3,2,1,0:T(8,128)(2,1)}, u32[]{:S(2)}) copy-start(bf16[3,3,64,64]{3,2,1,0:T(8,128)(2,1)} %get-tuple-element.143) | copy-start | bytes 221188
  109.8 5.6 %collective-permute-start.1 = (bf16[1,16,16,128]{3,2,1,0:T(8,128)(2,1)S(1)}, bf16[1,16,16,128]{3,2,1,0:T(8,128)(2,1)S(1)}, u32[]{:S(2)}, u32[]{:S(2)}) collective-permute-start(bf16[1,16,16,128]{3,2,1,0:T(8,128)(2,1)S(1)} %slice.770), channel_id=1, source_target_pairs={{4,0},{8,4},{12,8},{16,12},{20,16},{24,20},{28,24},{5,1},{9,5},{13... | collective-permute-start | bytes 196616 | tf_op jit(solution)/shard_map/ppermute | solution.py:19
  115.4 4.3 %collective-permute-start.2 = (bf16[18,1,16,128]{3,2,1,0:T(8,128)(2,1)S(1)}, bf16[18,1,16,128]{3,2,1,0:T(8,128)(2,1)S(1)}, u32[]{:S(2)}, u32[]{:S(2)}) collective-permute-start(bf16[18,1,16,128]{3,2,1,0:T(8,128)(2,1)S(1)} %get-tuple-element.133), channel_id=1, source_target_pairs={{0,1},{1,2},{2,3},{4,5},{5,6},{6,7},{8,9},{9,10},{10,11},{12,13},{... | collective-permute-start | bytes 221192 | tf_op jit(solution)/shard_map/ppermute | solution.py:17
  117.5 5.1 %collective-permute-start.3 = (bf16[18,1,16,128]{3,2,1,0:T(8,128)(2,1)S(1)}, bf16[18,1,16,128]{3,2,1,0:T(8,128)(2,1)S(1)}, u32[]{:S(2)}, u32[]{:S(2)}) collective-permute-start(bf16[18,1,16,128]{3,2,1,0:T(8,128)(2,1)S(1)} %get-tuple-element.134), channel_id=1, source_target_pairs={{1,0},{2,1},{3,2},{5,4},{6,5},{7,6},{9,8},{10,9},{11,10},{13,12},{... | collective-permute-start | bytes 221192 | tf_op jit(solution)/shard_map/ppermute | solution.py:19
  124.3 1.2 copy-start.8
  132.3 1.0 copy-start.9
  135.2 6.0 %collective-permute-start.4 = (bf16[1,16,16,128]{3,2,1,0:T(8,128)(2,1)S(1)}, bf16[1,16,16,128]{3,2,1,0:T(8,128)(2,1)S(1)}, u32[]{:S(2)}, u32[]{:S(2)}) collective-permute-start(bf16[1,16,16,128]{3,2,1,0:T(8,128)(2,1)S(1)} %get-tuple-element.135), channel_id=1, source_target_pairs={{0,4},{4,8},{8,12},{12,16},{16,20},{20,24},{24,28},{1,5},{5,9},{9,... | collective-permute-start | bytes 196616 | tf_op jit(solution)/shard_map/ppermute | solution.py:17
  138.5 5.6 %collective-permute-start.5 = (bf16[1,16,16,128]{3,2,1,0:T(8,128)(2,1)S(1)}, bf16[1,16,16,128]{3,2,1,0:T(8,128)(2,1)S(1)}, u32[]{:S(2)}, u32[]{:S(2)}) collective-permute-start(bf16[1,16,16,128]{3,2,1,0:T(8,128)(2,1)S(1)} %get-tuple-element.136), channel_id=1, source_target_pairs={{4,0},{8,4},{12,8},{16,12},{20,16},{24,20},{28,24},{5,1},{9,5},{13... | collective-permute-start | bytes 196616 | tf_op jit(solution)/shard_map/ppermute | solution.py:19
  144.1 4.5 %collective-permute-start.6 = (bf16[18,1,16,128]{3,2,1,0:T(8,128)(2,1)S(1)}, bf16[18,1,16,128]{3,2,1,0:T(8,128)(2,1)S(1)}, u32[]{:S(2)}, u32[]{:S(2)}) collective-permute-start(bf16[18,1,16,128]{3,2,1,0:T(8,128)(2,1)S(1)} %get-tuple-element.131), channel_id=1, source_target_pairs={{0,1},{1,2},{2,3},{4,5},{5,6},{6,7},{8,9},{9,10},{10,11},{12,13},{... | collective-permute-start | bytes 221192 | tf_op jit(solution)/shard_map/ppermute | solution.py:17
  146.4 5.1 %collective-permute-start.7 = (bf16[18,1,16,128]{3,2,1,0:T(8,128)(2,1)S(1)}, bf16[18,1,16,128]{3,2,1,0:T(8,128)(2,1)S(1)}, u32[]{:S(2)}, u32[]{:S(2)}) collective-permute-start(bf16[18,1,16,128]{3,2,1,0:T(8,128)(2,1)S(1)} %get-tuple-element.132), channel_id=1, source_target_pairs={{1,0},{2,1},{3,2},{5,4},{6,5},{7,6},{9,8},{10,9},{11,10},{13,12},{... | collective-permute-start | bytes 221192 | tf_op jit(solution)/shard_map/ppermute | solution.py:19
  172.7 6.2 %copy-start.1 = (bf16[16,16,16,128]{3,2,1,0:T(8,128)(2,1)}, bf16[16,16,16,128]{3,2,1,0:T(8,128)(2,1)S(1)}, u32[]{:S(2)}) copy-start(bf16[16,16,16,128]{3,2,1,0:T(8,128)(2,1)S(1)} %multiply_convert_fusion) | copy-start | bytes 3145732
  172.8 6.1 %copy-start.10 = (bf16[2,2,2,2,128,128]{5,4,3,2,1,0:T(8,128)(2,1)S(1)}, bf16[2,2,2,2,128,128]{5,4,3,2,1,0:T(8,128)(2,1)}, u32[]{:S(2)}) copy-start(bf16[2,2,2,2,128,128]{5,4,3,2,1,0:T(8,128)(2,1)} %param.16) | copy-start | bytes 1572868
  172.8 6.1 %copy-start.12 = (f32[2,2,4]{2,1,0:T(2,128)S(1)}, f32[2,2,4]{2,1,0:T(2,128)}, u32[]{:S(2)}) copy-start(f32[2,2,4]{2,1,0:T(2,128)} %copy-done.11) | copy-start | bytes 196
  172.8 13.4 %copy-start.3 = (bf16[3,3,3,128,128]{4,3,2,1,0:T(8,128)(2,1)S(1)}, bf16[3,3,3,128,128]{4,3,2,1,0:T(8,128)(2,1)}, u32[]{:S(2)}) copy-start(bf16[3,3,3,128,128]{4,3,2,1,0:T(8,128)(2,1)} %get-tuple-element.124) | copy-start | bytes 2654212
  173.5 5.7 %collective-permute-start.8 = (bf16[1,8,16,128]{3,2,1,0:T(8,128)(2,1)S(1)}, bf16[1,8,16,128]{3,2,1,0:T(8,128)(2,1)S(1)}, u32[]{:S(2)}, u32[]{:S(2)}) collective-permute-start(bf16[1,8,16,128]{3,2,1,0:T(8,128)(2,1)S(1)} %get-tuple-element.151), channel_id=1, source_target_pairs={{0,4},{4,8},{8,12},{12,16},{16,20},{20,24},{24,28},{1,5},{5,9},{9,... | collective-permute-start | bytes 98312 | tf_op jit(solution)/shard_map/ppermute | solution.py:17
  176.9 5.5 %collective-permute-start.9 = (bf16[1,8,16,128]{3,2,1,0:T(8,128)(2,1)S(1)}, bf16[1,8,16,128]{3,2,1,0:T(8,128)(2,1)S(1)}, u32[]{:S(2)}, u32[]{:S(2)}) collective-permute-start(bf16[1,8,16,128]{3,2,1,0:T(8,128)(2,1)S(1)} %get-tuple-element.152), channel_id=1, source_target_pairs={{4,0},{8,4},{12,8},{16,12},{20,16},{24,20},{28,24},{5,1},{9,5},{13... | collective-permute-start | bytes 98312 | tf_op jit(solution)/shard_map/ppermute | solution.py:19
  182.4 4.2 %collective-permute-start.10 = (bf16[10,1,16,128]{3,2,1,0:T(8,128)(2,1)S(1)}, bf16[10,1,16,128]{3,2,1,0:T(8,128)(2,1)S(1)}, u32[]{:S(2)}, u32[]{:S(2)}) collective-permute-start(bf16[10,1,16,128]{3,2,1,0:T(8,128)(2,1)S(1)} %get-tuple-element.149), channel_id=1, source_target_pairs={{0,1},{1,2},{2,3},{4,5},{5,6},{6,7},{8,9},{9,10},{10,11},{12,13},{... | collective-permute-start | bytes 122888 | tf_op jit(solution)/shard_map/ppermute | solution.py:17
  184.6 4.7 %collective-permute-start.11 = (bf16[10,1,16,128]{3,2,1,0:T(8,128)(2,1)S(1)}, bf16[10,1,16,128]{3,2,1,0:T(8,128)(2,1)S(1)}, u32[]{:S(2)}, u32[]{:S(2)}) collective-permute-start(bf16[10,1,16,128]{3,2,1,0:T(8,128)(2,1)S(1)} %get-tuple-element.150), channel_id=1, source_target_pairs={{1,0},{2,1},{3,2},{5,4},{6,5},{7,6},{9,8},{10,9},{11,10},{13,12},{... | collective-permute-start | bytes 122888 | tf_op jit(solution)/shard_map/ppermute | solution.py:19
  195.0 13.1 %copy-start.2 = (bf16[3,3,3,128,128]{4,3,2,1,0:T(8,128)(2,1)S(1)}, bf16[3,3,3,128,128]{4,3,2,1,0:T(8,128)(2,1)}, u32[]{:S(2)}) copy-start(bf16[3,3,3,128,128]{4,3,2,1,0:T(8,128)(2,1)} %get-tuple-element.126) | copy-start | bytes 2654212
  195.8 5.8 %collective-permute-start.12 = (bf16[1,4,8,128]{3,2,1,0:T(8,128)(2,1)S(1)}, bf16[1,4,8,128]{3,2,1,0:T(8,128)(2,1)S(1)}, u32[]{:S(2)}, u32[]{:S(2)}) collective-permute-start(bf16[1,4,8,128]{3,2,1,0:T(8,128)(2,1)S(1)} %get-tuple-element.155), channel_id=1, source_target_pairs={{0,4},{4,8},{8,12},{12,16},{16,20},{20,24},{24,28},{1,5},{5,9},{9,... | collective-permute-start | bytes 24584 | tf_op jit(solution)/shard_map/ppermute | solution.py:17
  199.6 5.3 %collective-permute-start.13 = (bf16[1,4,8,128]{3,2,1,0:T(8,128)(2,1)S(1)}, bf16[1,4,8,128]{3,2,1,0:T(8,128)(2,1)S(1)}, u32[]{:S(2)}, u32[]{:S(2)}) collective-permute-start(bf16[1,4,8,128]{3,2,1,0:T(8,128)(2,1)S(1)} %get-tuple-element.156), channel_id=1, source_target_pairs={{4,0},{8,4},{12,8},{16,12},{20,16},{24,20},{28,24},{5,1},{9,5},{13... | collective-permute-start | bytes 24584 | tf_op jit(solution)/shard_map/ppermute | solution.py:19
  204.9 3.4 %collective-permute-start.14 = (bf16[6,1,8,128]{3,2,1,0:T(8,128)(2,1)S(1)}, bf16[6,1,8,128]{3,2,1,0:T(8,128)(2,1)S(1)}, u32[]{:S(2)}, u32[]{:S(2)}) collective-permute-start(bf16[6,1,8,128]{3,2,1,0:T(8,128)(2,1)S(1)} %get-tuple-element.153), channel_id=1, source_target_pairs={{0,1},{1,2},{2,3},{4,5},{5,6},{6,7},{8,9},{9,10},{10,11},{12,13},{... | collective-permute-start | bytes 36872 | tf_op jit(solution)/shard_map/ppermute | solution.py:17
  206.9 4.4 %collective-permute-start.15 = (bf16[6,1,8,128]{3,2,1,0:T(8,128)(2,1)S(1)}, bf16[6,1,8,128]{3,2,1,0:T(8,128)(2,1)S(1)}, u32[]{:S(2)}, u32[]{:S(2)}) collective-permute-start(bf16[6,1,8,128]{3,2,1,0:T(8,128)(2,1)S(1)} %get-tuple-element.154), channel_id=1, source_target_pairs={{1,0},{2,1},{3,2},{5,4},{6,5},{7,6},{9,8},{10,9},{11,10},{13,12},{... | collective-permute-start | bytes 36872 | tf_op jit(solution)/shard_map/ppermute | solution.py:19
  213.1 8.1 %copy-start.4 = (bf16[3,3,3,128,128]{4,3,2,1,0:T(8,128)(2,1)S(1)}, bf16[3,3,3,128,128]{4,3,2,1,0:T(8,128)(2,1)}, u32[]{:S(2)}) copy-start(bf16[3,3,3,128,128]{4,3,2,1,0:T(8,128)(2,1)} %get-tuple-element.125) | copy-start | bytes 2654212
  215.4 5.9 %collective-permute-start.16 = (bf16[1,2,4,128]{3,2,1,0:T(4,128)(2,1)S(1)}, bf16[1,2,4,128]{3,2,1,0:T(4,128)(2,1)S(1)}, u32[]{:S(2)}, u32[]{:S(2)}) collective-permute-start(bf16[1,2,4,128]{3,2,1,0:T(4,128)(2,1)S(1)} %get-tuple-element.159), channel_id=1, source_target_pairs={{0,4},{4,8},{8,12},{12,16},{16,20},{20,24},{24,28},{1,5},{5,9},{9,... | collective-permute-start | bytes 6152 | tf_op jit(solution)/shard_map/ppermute | solution.py:17
  219.2 5.0 %collective-permute-start.17 = (bf16[1,2,4,128]{3,2,1,0:T(4,128)(2,1)S(1)}, bf16[1,2,4,128]{3,2,1,0:T(4,128)(2,1)S(1)}, u32[]{:S(2)}, u32[]{:S(2)}) collective-permute-start(bf16[1,2,4,128]{3,2,1,0:T(4,128)(2,1)S(1)} %get-tuple-element.160), channel_id=1, source_target_pairs={{4,0},{8,4},{12,8},{16,12},{20,16},{24,20},{28,24},{5,1},{9,5},{13... | collective-permute-start | bytes 6152 | tf_op jit(solution)/shard_map/ppermute | solution.py:19
  224.3 3.4 %collective-permute-start.18 = (bf16[4,1,4,128]{3,2,1,0:T(4,128)(2,1)S(1)}, bf16[4,1,4,128]{3,2,1,0:T(4,128)(2,1)S(1)}, u32[]{:S(2)}, u32[]{:S(2)}) collective-permute-start(bf16[4,1,4,128]{3,2,1,0:T(4,128)(2,1)S(1)} %get-tuple-element.157), channel_id=1, source_target_pairs={{0,1},{1,2},{2,3},{4,5},{5,6},{6,7},{8,9},{9,10},{10,11},{12,13},{... | collective-permute-start | bytes 12296 | tf_op jit(solution)/shard_map/ppermute | solution.py:17
  226.2 4.4 %collective-permute-start.19 = (bf16[4,1,4,128]{3,2,1,0:T(4,128)(2,1)S(1)}, bf16[4,1,4,128]{3,2,1,0:T(4,128)(2,1)S(1)}, u32[]{:S(2)}, u32[]{:S(2)}) collective-permute-start(bf16[4,1,4,128]{3,2,1,0:T(4,128)(2,1)S(1)} %get-tuple-element.158), channel_id=1, source_target_pairs={{1,0},{2,1},{3,2},{5,4},{6,5},{7,6},{9,8},{10,9},{11,10},{13,12},{... | collective-permute-start | bytes 12296 | tf_op jit(solution)/shard_map/ppermute | solution.py:19
where the time goes:
time: 237 us; the launch traced here: 235 us
  matrix products  105 us (44%)
  starting transfers between devices  57.4 us (24%)
  waiting for transfers between devices  33.5 us (14%)
  local copies, waits for them, and re-layouts  27 us (11%)
  other arithmetic  10.2 us (4%)
    dot_general x4, matrix products, add_block(): jnp.dot(one_hot, rows_here, preferred_element_type=jnp.float32)  60.5 us
    ppermute x10, waiting for transfers between devices, with_halo(): lax.ppermute(head, axis, [((i + 1) % count, i) for i in range(ends)])  29.2 us
    ppermute x10, starting transfers between devices, with_halo(): lax.ppermute(tail, axis, [(i, (i + 1) % count) for i in range(ends)])  27.7 us
    dot_general x18, matrix products, leaf_sweep(): jnp.einsum('xyzk,kc->xyzc', window, tap_table[step_x, step_y], preferred_...  27.4 us
    ppermute x10, starting transfers between devices, with_halo(): lax.ppermute(head, axis, [((i + 1) % count, i) for i in range(ends)])  16.8 us
    dot_general x81, matrix products, coarse_layer(): jnp.einsum('xyzk,kc->xyzc', window, kernel[step_x, step_y, step_z], prefe...  13.9 us
    unnamed x38, local copies, waits for them, and re-layouts  9.11 us
    all_to_all x1, starting transfers between devices, per_device(): lax.all_to_all(outgoing, ('gx', 'gy'), split_axis=0, concat_axis=0, tiled...  7.1 us
  transfers between devices with their start and end apart: 22, of which 11 were waited for; matrix products, arithmetic and copies ran while one was open for 12% of the time, Pallas kernels for 0%

commit v1 on v0

v1 whole, which is shorter than its diff:
```python
import functools

import jax
import jax.numpy as jnp
from jax import lax
from jax.experimental import pallas as pl
from jax.experimental.pallas import tpu as pltpu
from jax.sharding import PartitionSpec as P

BRICK = 8
F32 = jnp.float32
BF16 = jnp.bfloat16
SIDES = [(-1, 0), (1, 0), (0, -1), (0, 1), (-1, -1), (-1, 1), (1, -1), (1, 1)]


def dot(left, right):
    return jnp.dot(left, right, preferred_element_type=F32)


def leaf_taps(kernels):
    low, mid, high = kernels[:, :, :, 0], kernels[:, :, :, 1], kernels[:, :, :, 2]
    none = jnp.zeros_like(low)
    first = jnp.concatenate([mid, high, none, low], -2)
    second = jnp.concatenate([low, mid, high, none], -2)
    taps = jnp.concatenate([first, second], -1)
    return taps.reshape(taps.shape[0], 9, taps.shape[3], taps.shape[4])


def lift_blocks(lift_weight, copies):
    feature_count, channels = lift_weight.shape
    tiled = jnp.tile(lift_weight, (copies, copies))
    row = lax.broadcasted_iota(jnp.int32, tiled.shape, 0) // feature_count
    column = lax.broadcasted_iota(jnp.int32, tiled.shape, 1) // channels
    return jnp.where(row == column, tiled, 0)


def spread(mask, factor, factor_z, pad_z=0):
    wide = jnp.repeat(jnp.repeat(mask, factor, 0), factor, 1)
    wide = jnp.repeat(wide, factor_z, 2).astype(F32)
    wide = jnp.pad(wide, ((0, 0), (0, 0), (0, pad_z)))
    return jnp.broadcast_to(wide[..., None], wide.shape + (128,))


def side_parts(count, here, other):
    near, far = 1, count
    own = {-1: near, 1: far, 0: pl.ds(1, count)}
    there = {-1: count + 1, 1: 0, 0: pl.ds(1, count)}
    return (own[here], own[other]), (there[here], there[other])


class Halo:
    def __init__(self, size_x, size_y, send_sems, recv_sems):
        self.place_x, self.place_y = lax.axis_index("gx"), lax.axis_index("gy")
        self.size_x, self.size_y = size_x, size_y
        self.send_sems, self.recv_sems = send_sems, recv_sems

    def each(self, action):
        for index, (step_x, step_y) in enumerate(SIDES):
            to_x, to_y = self.place_x + step_x, self.place_y + step_y
            tests = []
            if step_x:
                tests.append(to_x >= 0 if step_x < 0 else to_x < self.size_x)
            if step_y:
                tests.append(to_y >= 0 if step_y < 0 else to_y < self.size_y)
            exists = tests[0] if len(tests) == 1 else jnp.logical_and(*tests)

            @pl.when(exists)
            def _():
                action(index, step_x, step_y, (to_x, to_y))

    def barrier(self):
        semaphore = pltpu.get_barrier_semaphore()

        def signal(index, step_x, step_y, target):
            pl.semaphore_signal(
                semaphore, inc=1, device_id=target, device_id_type=pl.DeviceIdType.MESH
            )

        def near(place, size):
            before = jnp.where(place > 0, 1, 0)
            return before + jnp.where(place < size - 1, 1, 0)

        self.each(signal)
        columns = near(self.place_x, self.size_x) + 1
        pl.semaphore_wait(semaphore, columns * (near(self.place_y, self.size_y) + 1) - 1)

    def copy(self, stage, buffer, index, step_x, step_y, target):
        source, landing = side_parts(buffer.shape[0] - 2, step_x, step_y)
        return pltpu.make_async_remote_copy(
            src_ref=buffer.at[source],
            dst_ref=buffer.at[landing],
            send_sem=self.send_sems.at[stage, index],
            recv_sem=self.recv_sems.at[stage, index],
            device_id=target,
            device_id_type=pl.DeviceIdType.MESH,
        )

    def start(self, stage, buffer):
        self.each(lambda *where: self.copy(stage, buffer, *where).start())

    def wait_arrived(self, stage, buffer):
        def arrived(index, step_x, step_y, target):
            opposite = SIDES.index((-step_x, -step_y))
            self.copy(stage, buffer, opposite, -step_x, -step_y, target).wait_recv()

        self.each(arrived)

    def wait_sent(self, stage, buffer):
        self.each(lambda *where: self.copy(stage, buffer, *where).wait_send())


def clear_border(buffer):
    last = buffer.shape[0] - 1
    edge = jnp.zeros(buffer.shape[1:], buffer.dtype)
    column = jnp.zeros((buffer.shape[0],) + buffer.shape[2:], buffer.dtype)
    buffer[0] = edge
    buffer[last] = edge
    buffer[:, 0] = column
    buffer[:, last] = column


def shift_rows(rows, period):
    count = rows.shape[0]
    z = lax.broadcasted_iota(jnp.int32, rows.shape, 0) % period
    before = jnp.where(z == 0, 0.0, pltpu.roll(rows, 1, 0))
    after = jnp.where(z == period - 1, 0.0, pltpu.roll(rows, count - 1, 0))
    return before, after


def store_leaf(buffer, at_x, at_y, rows, shape):
    before, after = shift_rows(rows, shape[2])
    lane = lax.broadcasted_iota(jnp.int32, rows.shape, 1)
    outer = jnp.where(lane < rows.shape[1] // 2, after, before)
    both = jnp.concatenate([rows, outer], -1).astype(BF16)
    buffer[at_x, at_y] = both.reshape(shape[:3] + (both.shape[-1],))


def stacked_z(values):
    shape = values.shape
    rows = values.reshape(-1, shape[-1])
    before, after = shift_rows(rows, shape[2])
    return jnp.concatenate([before, rows, after], -1).reshape(shape[:3] + (3 * shape[3],))


def pair_part(values, part_x, part_y):
    size_x, size_y = values.shape[:2]
    split = values.reshape((size_x // 2, 2, size_y // 2, 2) + values.shape[2:])
    return split[:, part_x, :, part_y]


def encoder(
    n_gx,
    n_gy,
    arrived,
    slots,
    lift,
    taps,
    down_leaf,
    down_coarse,
    coarse_convs,
    occ0,
    occ1,
    occ2,
    occ3,
    leaf_out,
    top_out,
    summed,
    leaf_a,
    leaf_b,
    coarse_a,
    coarse_b,
    coarse_c,
    stacked,
    level_one,
    level_two,
    send_sems,
    recv_sems,
):
    halo = Halo(n_gx, n_gy, send_sems, recv_sems)
    for buffer in (leaf_a, leaf_b, coarse_a, coarse_b, coarse_c):
        clear_border(buffer)
    halo.barrier()

    senders, slot_rows, width = arrived.shape
    cap = slots.shape[1]
    lanes = cap // slot_rows
    features = width // lanes
    span = summed.shape[1]
    rows_hi = summed.shape[0]
    group = 4
    order_from = lax.broadcasted_iota(jnp.int32, (cap, cap), 0)
    order_to = lax.broadcasted_iota(jnp.int32, (cap, cap), 1)
    order = jnp.where(
        order_from == (order_to % slot_rows) * lanes + order_to // slot_rows, 1.0, 0.0
    ).astype(BF16)
    pick_from = lax.broadcasted_iota(jnp.int32, (width, lanes * span), 0)
    pick_to = lax.broadcasted_iota(jnp.int32, (width, lanes * span), 1)
    pick = jnp.where(
        pick_from == (pick_to // span) * features + pick_to % features, 1.0, 0.0
    ).astype(BF16)
    column_group = (
        lax.broadcasted_iota(jnp.int32, (cap, span), 1) // features
    ).astype(F32)
    row_index = lax.broadcasted_iota(jnp.int32, (rows_hi, cap), 0).astype(F32)
    summed[...] = jnp.zeros_like(summed)

    def add_group(step, carry):
        base = pl.multiple_of(step * 8, 8)
        index = slots[pl.ds(base, 8), :]
        half = index // 2
        high = half % rows_hi
        low = (index // (2 * rows_hi)) * 2 + index % 2
        high_row = 64.0 * dot((high // 64).astype(F32).astype(BF16), order) + dot(
            (high % 64).astype(F32).astype(BF16), order
        )
        low_column = lax.dot_general(
            order,
            low.astype(F32).astype(BF16),
            (((0,), (1,)), ((), ())),
            preferred_element_type=F32,
        )
        for part in range(8 // group):
            hots, tables = [], []
            for inner in range(group):
                place = part * group + inner
                hot = jnp.where(row_index == high_row[place : place + 1], 1.0, 0.0)
                hots.append(hot.astype(BF16))
                wide = dot(arrived[base + place], pick)
                wide = jnp.concatenate(
                    [wide[:, lane * span : (lane + 1) * span] for lane in range(lanes)], 0
                )
                tables.append(
                    jnp.where(column_group == low_column[:, place : place + 1], wide, 0.0).astype(
                        BF16
                    )
                )
            summed[...] += dot(jnp.concatenate(hots, 1), jnp.concatenate(tables, 0))
        return carry

    lax.fori_loop(0, senders // 8, add_group, 0)

    size_x, size_y, size_z, leaf_width = leaf_out.shape
    quarter = rows_hi // (size_y * size_z)
    rest = summed[...]
    lifted = 0.0
    for piece in range(3):
        cut = rest.astype(BF16)
        rest = rest - cut.astype(F32)
        lifted = lifted + dot(cut, lift[...])
    inside_y = pl.ds(1, size_y)
    for block in range(size_x // quarter):
        store_leaf(
            leaf_a,
            pl.ds(1 + block * quarter, quarter),
            inside_y,
            lifted[:, block * leaf_width : (block + 1) * leaf_width],
            (quarter, size_y, size_z),
        )

    halo.start(0, leaf_a)

    def convolve(source, layer, x, count_x, y, count_y):
        total = None
        for step in range(9):
            window = source[pl.ds(x + step // 3, count_x), pl.ds(y + step % 3, count_y)]
            term = dot(window.reshape(-1, window.shape[-1]), taps[layer, step])
            total = term if total is None else total + term
        return jnp.maximum(total, 0.0)

    def leaf_layer(source, layer, emit):
        def block(x, count_x, y, count_y):
            swept = convolve(source, layer, x, count_x, y, count_y)
            occupied = jnp.concatenate(
                [
                    occ0[pl.ds((x + step) // BRICK, 1), y : y + count_y]
                    for step in range(count_x)
                ],
                0,
            )
            emit(x, count_x, y, count_y, swept * occupied.reshape(swept.shape))

        def inner(step, carry):
            block(1 + 2 * step, 2, 1, size_y - 2)
            return carry

        lax.fori_loop(0, (size_x - 2) // 2, inner, 0)
        halo.wait_arrived(layer, source)
        block(0, 1, 0, size_y)
        block(size_x - 1, 1, 0, size_y)
        block(1, size_x - 2, 0, 1)
        block(1, size_x - 2, size_y - 1, 1)

    def keep_first(x, count_x, y, count_y, rows):
        store_leaf(
            leaf_b,
            pl.ds(1 + x, count_x),
            pl.ds(1 + y, count_y),
            rows,
            (count_x, count_y, size_z),
        )

    def keep_second(x, count_x, y, count_y, rows):
        leaf_out[pl.ds(x, count_x), pl.ds(y, count_y)] = rows.astype(BF16).reshape(
            count_x, count_y, size_z, leaf_width
        )

    leaf_layer(leaf_a, 0, keep_first)
    halo.start(1, leaf_b)
    leaf_layer(leaf_b, 1, keep_second)

    def coarse_conv(level, kernel, occupied):
        count, depth = kernel.shape[0] - 2, kernel.shape[2]
        total = None
        for step in range(9):
            step_x, step_y = step // 3, step % 3
            window = kernel[step_x : step_x + count, step_y : step_y + count]
            window = window.reshape(count * count * depth, window.shape[-1]).astype(BF16)
            term = dot(window, coarse_convs[level, step])
            total = term if total is None else total + term
        return jnp.maximum(total, 0.0).reshape(occupied.shape) * occupied[...]

    def finish_down(stage, buffer, total, occupied):
        count = occupied.shape[0]
        cells = jnp.maximum(total, 0.0).reshape(occupied.shape) * occupied[...]
        buffer[1 : count + 1, 1 : count + 1] = cells
        halo.start(stage, buffer)
        halo.wait_arrived(stage, buffer)

    total = 0.0
    leaf = leaf_out[...]
    for part in range(4):
        piece = pair_part(leaf, part // 2, part % 2)
        total = total + dot(piece.reshape(-1, leaf_width), down_leaf[part])
    finish_down(2, coarse_a, total, occ1)
    stacked[...] = stacked_z(coarse_a[...]).astype(BF16)
    level_one[...] = coarse_conv(0, stacked, occ1)

    def shrink(level, source, depth):
        total = 0.0
        for part_z in range(2):
            half = source[:, :, pl.ds(part_z, depth, 2), :]
            for part in range(4):
                piece = pair_part(half, part // 2, part % 2)
                piece = piece.reshape(-1, piece.shape[-1]).astype(BF16)
                total = total + dot(piece, down_coarse[level, 2 * part + part_z])
        return total

    finish_down(3, coarse_b, shrink(0, level_one, occ2.shape[2]), occ2)
    deep = occ2.shape[2]
    level_two[:, :, deep : 2 * deep] = jnp.zeros_like(occ2)
    level_two[:, :, 0:deep] = coarse_conv(1, stacked_z(coarse_b[...]), occ2)
    finish_down(4, coarse_c, shrink(1, level_two, occ3.shape[2]), occ3)
    top_out[...] = coarse_conv(2, stacked_z(coarse_c[...]), occ3)

    for stage, buffer in enumerate((leaf_a, leaf_b, coarse_a, coarse_b, coarse_c)):
        halo.wait_sent(stage, buffer)


def per_device(
    n_gx,
    n_gy,
    records,
    slot_voxels,
    brick_mask,
    lift_weight,
    leaf_convs,
    down_leaf,
    down_coarse,
    coarse_convs,
):
    arrived = lax.all_to_all(records[0], ("gx", "gy"), split_axis=0, concat_axis=0, tiled=True)
    slots = lax.all_to_all(slot_voxels[0], ("gx", "gy"), split_axis=0, concat_axis=0, tiled=True)
    bricks_x, bricks_y, bricks_z = brick_mask.shape
    size_x, size_y, size_z = BRICK * bricks_x, BRICK * bricks_y, BRICK * bricks_z // 2
    features, channels = lift_weight.shape
    wide = down_leaf.shape[-1]
    rows_hi = size_x * size_y * size_z // 4
    span = 8 * features
    occ0 = spread(jnp.repeat(brick_mask, BRICK, 1), 1, BRICK // 2)
    occ1 = spread(brick_mask, BRICK // 2, BRICK // 2)
    occ2 = spread(brick_mask, BRICK // 4, BRICK // 4)
    occ3 = spread(brick_mask, 1, 1, 4)
    vmem = pl.BlockSpec(memory_space=pltpu.VMEM)
    leaf, top = pl.pallas_call(
        functools.partial(encoder, n_gx, n_gy),
        out_shape=(
            jax.ShapeDtypeStruct((size_x, size_y, size_z, 2 * channels), BF16),
            jax.ShapeDtypeStruct(occ3.shape, F32),
        ),
        in_specs=[vmem] * 11,
        out_specs=(vmem, vmem),
        scratch_shapes=[
            pltpu.VMEM((rows_hi, span), F32),
            pltpu.VMEM((size_x + 2, size_y + 2, size_z, 4 * channels), BF16),
            pltpu.VMEM((size_x + 2, size_y + 2, size_z, 4 * channels), BF16),
            pltpu.VMEM((size_x // 2 + 2, size_y // 2 + 2, size_z, wide), F32),
            pltpu.VMEM((size_x // 4 + 2, size_y // 4 + 2, size_z // 2, wide), F32),
            pltpu.VMEM((size_x // 8 + 2, size_y // 8 + 2, size_z // 2, wide), F32),
            pltpu.VMEM((size_x // 2 + 2, size_y // 2 + 2, size_z, 3 * wide), BF16),
            pltpu.VMEM((size_x // 2, size_y // 2, size_z, wide), F32),
            pltpu.VMEM((size_x // 4, size_y // 4, size_z, wide), F32),
            pltpu.SemaphoreType.DMA((5, 8)),
            pltpu.SemaphoreType.DMA((5, 8)),
        ],
        compiler_params=pltpu.CompilerParams(
            collective_id=0, has_side_effects=True, vmem_limit_bytes=56 * 1024 * 1024
        ),
        cost_estimate=pl.CostEstimate(
            flops=30_000_000_000, bytes_accessed=10_000_000, transcendentals=0
        ),
    )(
        arrived,
        slots,
        lift_blocks(lift_weight, 8),
        leaf_taps(leaf_convs),
        down_leaf.reshape(4, 2 * channels, wide),
        down_coarse.reshape(2, 8, wide, wide),
        coarse_convs.reshape(3, 9, 3 * wide, wide),
        occ0,
        occ1,
        occ2,
        occ3,
    )
    return leaf, top[:, :, :bricks_z].astype(BF16)


def solution(mesh):
    in_specs = (
        P(("gx", "gy"), None, None, None),
        P(("gx", "gy"), None, None),
        P("gx", "gy", None),
        P(),
        P(),
        P(),
        P(),
        P(),
    )
    out_specs = (P("gx", "gy", None, None), P("gx", "gy", None, None))
    return jax.shard_map(
        functools.partial(per_device, mesh.shape["gx"], mesh.shape["gy"]),
        mesh=mesh,
        in_specs=in_specs,
        out_specs=out_specs,
        check_vma=False,
    )
```

time: 237 us -> 87.9 us (0.37)
  matrix products: 105 us -> 0 us
  starting transfers between devices: 57.4 us -> 10.1 us
  Pallas kernels: 0 us -> 46 us
  waiting for transfers between devices: 33.5 us -> 16 us
  local copies, waits for them, and re-layouts: 27 us -> 11.3 us
  other arithmetic: 10.2 us -> 3.3 us
    dot_general x107 -> x0, matrix products: 105 us -> none  [the longest x4 60.5 us: add_block(): jnp.dot(one_hot, rows_here, preferred_element_type=jnp.float32)]
    pallas_call x0 -> x1, Pallas kernels: none -> 46 us  [per_device(): pl.pallas_call(functools.partial(encoder, n_gx, n_gy), out_shape=(jax.Sha...]
    ppermute x20 -> x0, starting transfers between devices: 44.5 us -> none  [the longest x10 27.7 us: with_halo(): lax.ppermute(tail, axis, [(i, (i + 1) % count) for i in range(ends)])]
    ppermute x20 -> x0, waiting for transfers between devices: 29.2 us -> none  [the longest x10 29.2 us: with_halo(): lax.ppermute(head, axis, [((i + 1) % count, i) for i in range(ends)])]
    all_to_all x2, waiting for transfers between devices: 4.29 us -> 16 us  [the longest x1 12.1 us: per_device(): lax.all_to_all(records[0], ('gx', 'gy'), split_axis=0, concat_axis=0, til...]
    unnamed x38 -> x6, local copies, waits for them, and re-layouts: 9.11 us -> 3.03 us
    unnamed x5 -> x0, other arithmetic: 4.99 us -> none
    squeeze x4 -> x1, local copies, waits for them, and re-layouts: 4.95 us -> 0.08 us  [leaf_taps(): kernels[:, :, :, 0]]
  transfers between devices with their start and end apart: 22 -> 2, of which waited for: 11 -> 2; matrix products, arithmetic and copies ran while one was open for 12% -> 7% of each run, Pallas kernels for 0% -> 0%
where the time goes in v1:
time: 87.9 us; the launch traced here: 87.4 us
  Pallas kernels  46 us (52%)
  waiting for transfers between devices  16 us (18%)
  local copies, waits for them, and re-layouts  11.3 us (13%)
  starting transfers between devices  10.1 us (11%)
  other arithmetic  3.3 us (4%)
    pallas_call x1, Pallas kernels, per_device(): pl.pallas_call(functools.partial(encoder, n_gx, n_gy), out_shape=(jax.Sha...  46 us
    all_to_all x1, waiting for transfers between devices, per_device(): lax.all_to_all(records[0], ('gx', 'gy'), split_axis=0, concat_axis=0, til...  12.1 us
    all_to_all x1, starting transfers between devices, per_device(): lax.all_to_all(slot_voxels[0], ('gx', 'gy'), split_axis=0, concat_axis=0,...  7.1 us
    all_to_all x1, waiting for transfers between devices, per_device(): lax.all_to_all(slot_voxels[0], ('gx', 'gy'), split_axis=0, concat_axis=0,...  3.92 us
    broadcast_in_dim x4, local copies, waits for them, and re-layouts, spread(): return jnp.broadcast_to(wide[..., None], wide.shape + (128,))  3.22 us
    unnamed x6, local copies, waits for them, and re-layouts  3.03 us
    all_to_all x1, starting transfers between devices, per_device(): lax.all_to_all(records[0], ('gx', 'gy'), split_axis=0, concat_axis=0, til...  3.01 us
  transfers between devices with their start and end apart: 2, of which 2 were waited for; matrix products, arithmetic and copies ran while one was open for 7% of the time, Pallas kernels for 0%

profile of v1, /device:TPU:1, one launch (start us, length us, event | category | flops | bytes accessed | tf_op | source)
XLA Modules:
  0.0 87.4 jit_solution(9183780695695936)
XLA Ops:
  0.6 0.0 copy-start
  0.6 1.5 %all_to_all.11 = s32[32,1,256]{2,1,0:T(1,128)} reshape(s32[1,32,256]{2,1,0:T(8,128)} %param.9) | data formatting | bytes 65536 | tf_op jit(solution)/shard_map/all_to_all | solution.py:372
  2.1 7.1 %all-to-all-start.1 = ((s32[32,1,256]{2,1,0:T(1,128)}), s32[32,1,256]{2,1,0:T(1,128)S(1)}, u32[]{:S(2)}, u32[]{:S(2)}) async-start(s32[32,1,256]{2,1,0:T(1,128)} %all_to_all.11), calls=%async_computation.1 | async-start | bytes 65536 | tf_op jit(solution)/shard_map/all_to_all | solution.py:372
  9.2 0.7 convert_element_type.55
  9.9 0.1 copy.41
  10.0 0.1 copy.39
  10.1 0.8 tile.4
  10.9 0.3 tile.10
  11.2 0.1 broadcast_in_dim.60
  11.3 0.1 convert_element_type.58
  11.4 0.1 copy.43
  11.5 0.1 copy.44
  11.5 0.1 broadcast_in_dim.57
  11.6 0.1 convert_element_type.56
  11.7 0.1 copy.40
  11.8 0.1 copy.45
  11.9 0.1 copy.46
  12.1 3.9 %all-to-all-done.1 = s32[32,1,256]{2,1,0:T(1,128)S(1)} async-done(((s32[32,1,256]{2,1,0:T(1,128)}), s32[32,1,256]{2,1,0:T(1,128)S(1)}, u32[]{:S(2)}, u32[]{:S(2)}) %all-to-all-start.1) | async-done | bytes 32800 | tf_op jit(solution)/shard_map/all_to_all | solution.py:372
  16.0 3.0 %all-to-all-start = ((bf16[32,64,128]{2,1,0:T(8,128)(2,1)}), bf16[32,64,128]{2,1,0:T(8,128)(2,1)S(1)}, u32[]{:S(2)}, u32[]{:S(2)}) async-start(bf16[32,64,128]{2,1,0:T(8,128)(2,1)} %bitcast.31), calls=%async_computation | async-start | bytes 1048576 | tf_op jit(solution)/shard_map/all_to_all | solution.py:371
  19.0 0.0 copy-done
  19.0 0.1 slice_bitcast_fusion
  19.1 0.1 broadcast_in_dim.56
  19.2 1.7 %maximum_maximum_fusion = bf16[2,3,3,256,128]{4,3,2,1,0:T(8,128)(2,1)} fusion(bf16[2,3,3,64,64]{4,3,2,1,0:T(8,128)(2,1)S(1)} %broadcast_in_dim.56, bf16[2,3,3,64,64]{4,3,2,1,0:T(8,128)(2,1)S(1)} %get-tuple-element.7, bf16[2,3,3,64,64]{4,3,2,1,0:T(8,128)(2,1)S(1)} %get-tuple-element.8, bf16[2,3,3,64,64]{4,3,2,1,0:T(8,128)(2,1)S(1)} %get-tuple-element.6), kind=kLoop, calls=%fused_computation | loop fusion | flops 9437184 | bytes 1769472 | tf_op jit(solution)/shard_map/concatenate | solution.py:25
  20.9 0.9 %fusion.lift = bf16[256,512]{1,0:T(8,128)(2,1)} fusion(bf16[256,512]{1,0:T(8,128)(2,1)S(1)} %tile.10, s32[512]{0:T(512)S(1)} %get-tuple-element.9, s32[512]{0:T(512)S(1)} %get-tuple-element.10, s32[256]{0:T(256)S(1)} %get-tuple-element.11, s32[256]{0:T(256)S(1)} %get-tuple-element.12, pred[256]{0:T(512)(128)(4,1)S(1)} %compare_and_fusion, ...), kind=kLoop, calls=%fused_computation.2 | loop fusion | flops 524288 | bytes 531200 | tf_op jit(solution)/shard_map/jit(_where)/select_n | solution.py:34
  21.8 0.6 copy.51
  22.4 12.1 %all-to-all-done.arrived = bf16[32,64,128]{2,1,0:T(8,128)(2,1)S(1)} async-done(((bf16[32,64,128]{2,1,0:T(8,128)(2,1)}), bf16[32,64,128]{2,1,0:T(8,128)(2,1)S(1)}, u32[]{:S(2)}, u32[]{:S(2)}) %all-to-all-start) | async-done | bytes 524320 | tf_op jit(solution)/shard_map/all_to_all | solution.py:371
  34.4 0.0 copy-start.1
  34.4 1.0 %broadcast_in_dim.63.occ1 = f32[8,8,16,128]{3,2,1,0:T(8,128)} broadcast(f32[8,8,16]{2,1,0:T(8,128)S(1)} %copy.44), dimensions={0,1,2} | broadcast | bytes 528384 | tf_op jit(solution)/shard_map/broadcast_in_dim | solution.py:41
  35.4 0.8 broadcast_in_dim.59.occ0
  36.3 0.7 broadcast_in_dim.67.occ2
  37.0 0.7 broadcast_in_dim.68.occ3
  37.6 0.0 copy-done.1
  37.6 46.0 %shard_map.95 = (bf16[16,16,16,128]{3,2,1,0:T(8,128)(2,1)}, f32[2,2,8,128]{3,2,1,0:T(8,128)}) custom-call(bf16[32,64,128]{2,1,0:T(8,128)(2,1)} %copy-done.1, s32[32,256]{1,0:T(8,128)} %bitcast.36, bf16[256,512]{1,0:T(8,128)(2,1)} %fusion.lift, bf16[2,9,256,128]{3,2,1,0:T(8,128)(2,1)} %bitcast.30, bf16[4,128,128]{2,1,0:T(8,128)(2,1)} %bitcast.41, ...), custom_call_target="tpu_custom_call" | custom-call | flops 30000001024 | bytes 10000000 | tf_op jit(solution)/shard_map/pallas_call | solution.py:384
  83.7 1.3 %slice.22 = bf16[2,2,4,128]{3,2,1,0:T(4,128)(2,1)} slice(f32[2,2,8,128]{3,2,1,0:T(8,128)} %get-tuple-element.5), slice={[0:2], [0:2], [0:4], [0:128]} | slice | bytes 8192 | tf_op jit(solution)/shard_map/slice | solution.py:424
  85.0 2.4 %copy.53 = bf16[16,16,16,128]{3,2,1,0:T(8,128)(2,1)} copy(bf16[16,16,16,128]{3,2,1,0:T(8,128)(2,1)} %get-tuple-element.15) | data formatting | bytes 2097152
  (12 shorter events, 0.1 us)
Async XLA Ops:
  0.6 18.4 %copy-start = (bf16[2,3,3,3,64,64]{5,4,3,2,1,0:T(8,128)(2,1)S(1)}, bf16[2,3,3,3,64,64]{5,4,3,2,1,0:T(8,128)(2,1)}, u32[]{:S(2)}) copy-start(bf16[2,3,3,3,64,64]{5,4,3,2,1,0:T(8,128)(2,1)} %param.12) | copy-start | bytes 1327108
  2.1 13.9 %all-to-all-start.1 = ((s32[32,1,256]{2,1,0:T(1,128)}), s32[32,1,256]{2,1,0:T(1,128)S(1)}, u32[]{:S(2)}, u32[]{:S(2)}) async-start(s32[32,1,256]{2,1,0:T(1,128)} %all_to_all.11), calls=%async_computation.1 | async-start | bytes 65536 | tf_op jit(solution)/shard_map/all_to_all | solution.py:372
  16.0 18.4 %all-to-all-start = ((bf16[32,64,128]{2,1,0:T(8,128)(2,1)}), bf16[32,64,128]{2,1,0:T(8,128)(2,1)S(1)}, u32[]{:S(2)}, u32[]{:S(2)}) async-start(bf16[32,64,128]{2,1,0:T(8,128)(2,1)} %bitcast.31), calls=%async_computation | async-start | bytes 1048576 | tf_op jit(solution)/shard_map/all_to_all | solution.py:371
  34.4 3.2 %copy-start.1 = (bf16[32,64,128]{2,1,0:T(8,128)(2,1)}, bf16[32,64,128]{2,1,0:T(8,128)(2,1)S(1)}, u32[]{:S(2)}) copy-start(bf16[32,64,128]{2,1,0:T(8,128)(2,1)S(1)} %all-to-all-done.arrived) | copy-start | bytes 1572868

commit v2 on v1

--- a/solution.py
+++ b/solution.py
@@ -15,30 +15,6 @@
 
 def dot(left, right):
     return jnp.dot(left, right, preferred_element_type=F32)
-
-
-def leaf_taps(kernels):
-    low, mid, high = kernels[:, :, :, 0], kernels[:, :, :, 1], kernels[:, :, :, 2]
-    none = jnp.zeros_like(low)
-    first = jnp.concatenate([mid, high, none, low], -2)
-    second = jnp.concatenate([low, mid, high, none], -2)
-    taps = jnp.concatenate([first, second], -1)
-    return taps.reshape(taps.shape[0], 9, taps.shape[3], taps.shape[4])
-
-
-def lift_blocks(lift_weight, copies):
-    feature_count, channels = lift_weight.shape
-    tiled = jnp.tile(lift_weight, (copies, copies))
-    row = lax.broadcasted_iota(jnp.int32, tiled.shape, 0) // feature_count
-    column = lax.broadcasted_iota(jnp.int32, tiled.shape, 1) // channels
-    return jnp.where(row == column, tiled, 0)
-
-
-def spread(mask, factor, factor_z, pad_z=0):
-    wide = jnp.repeat(jnp.repeat(mask, factor, 0), factor, 1)
-    wide = jnp.repeat(wide, factor_z, 2).astype(F32)
-    wide = jnp.pad(wide, ((0, 0), (0, 0), (0, pad_z)))
-    return jnp.broadcast_to(wide[..., None], wide.shape + (128,))
 
 
 def side_parts(count, here, other):
@@ -68,22 +44,6 @@
             def _():
                 action(index, step_x, step_y, (to_x, to_y))
 
-    def barrier(self):
-        semaphore = pltpu.get_barrier_semaphore()
-
-        def signal(index, step_x, step_y, target):
-            pl.semaphore_signal(
-                semaphore, inc=1, device_id=target, device_id_type=pl.DeviceIdType.MESH
-            )
-
-        def near(place, size):
-            before = jnp.where(place > 0, 1, 0)
-            return before + jnp.where(place < size - 1, 1, 0)
-
-        self.each(signal)
-        columns = near(self.place_x, self.size_x) + 1
-        pl.semaphore_wait(semaphore, columns * (near(self.place_y, self.size_y) + 1) - 1)
-
     def copy(self, stage, buffer, index, step_x, step_y, target):
         source, landing = side_parts(buffer.shape[0] - 2, step_x, step_y)
         return pltpu.make_async_remote_copy(
@@ -151,19 +111,22 @@
 def encoder(
     n_gx,
     n_gy,
+    records,
+    slots,
+    lift_weight,
+    leaf_convs,
+    down_leaf,
+    down_coarse_far,
+    coarse_convs_far,
+    occupied,
+    leaf_out,
+    top_out,
     arrived,
-    slots,
-    lift,
+    slots_out,
+    slots_in,
     taps,
-    down_leaf,
     down_coarse,
     coarse_convs,
-    occ0,
-    occ1,
-    occ2,
-    occ3,
-    leaf_out,
-    top_out,
     summed,
     leaf_a,
     leaf_b,
@@ -175,13 +138,96 @@
     level_two,
     send_sems,
     recv_sems,
+    owner_send_sems,
+    owner_recv_sems,
+    local_sems,
 ):
     halo = Halo(n_gx, n_gy, send_sems, recv_sems)
+    senders = n_gx * n_gy
+    me = halo.place_x * n_gy + halo.place_y
+    weights = (
+        pltpu.make_async_copy(down_coarse_far, down_coarse, local_sems.at[0]),
+        pltpu.make_async_copy(coarse_convs_far, coarse_convs, local_sems.at[1]),
+    )
+    own_records = pltpu.make_async_copy(records.at[me], arrived.at[0], local_sems.at[2])
+    own_records.start()
+
+    def owner(away):
+        index = lax.rem(me + away, senders)
+        return index, (index // n_gy, lax.rem(index, n_gy))
+
+    barrier = pltpu.get_barrier_semaphore()
+
+    def greet(away, carry):
+        pl.semaphore_signal(
+            barrier, inc=1, device_id=owner(away)[1], device_id_type=pl.DeviceIdType.MESH
+        )
+        return carry
+
     for buffer in (leaf_a, leaf_b, coarse_a, coarse_b, coarse_c):
         clear_border(buffer)
-    halo.barrier()
-
-    senders, slot_rows, width = arrived.shape
+    lax.fori_loop(1, senders, greet, 0)
+
+    def stage_slots(step, carry):
+        base = pl.multiple_of(step * 8, 8)
+        index = slots[pl.ds(base, 8), :]
+        for place in range(8):
+            slots_out[base + place] = index[place : place + 1]
+        return carry
+
+    lax.fori_loop(0, senders // 8, stage_slots, 0)
+    slots_in[0] = slots_out[me]
+    pl.semaphore_wait(barrier, senders - 1)
+
+    def owner_copies(away):
+        index, target = owner(away)
+        return (
+            pltpu.make_async_remote_copy(
+                src_ref=slots_out.at[index],
+                dst_ref=slots_in.at[away],
+                send_sem=owner_send_sems.at[0, away],
+                recv_sem=owner_recv_sems.at[0, away],
+                device_id=target,
+                device_id_type=pl.DeviceIdType.MESH,
+            ),
+            pltpu.make_async_remote_copy(
+                src_ref=records.at[index],
+                dst_ref=arrived.at[away],
+                send_sem=owner_send_sems.at[1, away],
+                recv_sem=owner_recv_sems.at[1, away],
+                device_id=target,
+                device_id_type=pl.DeviceIdType.MESH,
+            ),
+        )
+
+    def send_owner(away, carry):
+        for copy in owner_copies(away):
+            copy.start()
+        return carry
+
+    def owner_arrived(away, carry):
+        for copy in owner_copies(away):
+            copy.wait_recv()
+        return carry
+
+    def owner_sent(away, carry):
+        for copy in owner_copies(away):
+            copy.wait_send()
+        return carry
+
+    lax.fori_loop(1, senders, send_owner, 0)
+    for copy in weights:
+        copy.start()
+
+    for layer in range(2):
+        for step in range(9):
+            low, mid, high = (leaf_convs[layer, step, tap] for tap in range(3))
+            none = jnp.zeros_like(low)
+            first = jnp.concatenate([mid, high, none, low], 0)
+            second = jnp.concatenate([low, mid, high, none], 0)
+            taps[layer, step] = jnp.concatenate([first, second], 1)
+
+    slot_rows, width = arrived.shape[1:]
     cap = slots.shape[1]
     lanes = cap // slot_rows
     features = width // lanes
@@ -205,8 +251,10 @@
     summed[...] = jnp.zeros_like(summed)
 
     def add_group(step, carry):
-        base = pl.multiple_of(step * 8, 8)
-        index = slots[pl.ds(base, 8), :]
+        base = step * 8
+        lax.fori_loop(jnp.where(step > 0, base, 1), base + 8, owner_arrived, 0)
+        index = jnp.concatenate([slots_in[base + place] for place in range(8)], 0)
+        wide_all = dot(arrived[pl.ds(base, 8)].reshape(8 * slot_rows, width), pick)
         half = index // 2
         high = half % rows_hi
         low = (index // (2 * rows_hi)) * 2 + index % 2
@@ -225,7 +273,7 @@
                 place = part * group + inner
                 hot = jnp.where(row_index == high_row[place : place + 1], 1.0, 0.0)
                 hots.append(hot.astype(BF16))
-                wide = dot(arrived[base + place], pick)
+                wide = wide_all[place * slot_rows : (place + 1) * slot_rows]
                 wide = jnp.concatenate(
                     [wide[:, lane * span : (lane + 1) * span] for lane in range(lanes)], 0
                 )
@@ -237,16 +285,34 @@
             summed[...] += dot(jnp.concatenate(hots, 1), jnp.concatenate(tables, 0))
         return carry
 
+    own_records.wait()
     lax.fori_loop(0, senders // 8, add_group, 0)
 
     size_x, size_y, size_z, leaf_width = leaf_out.shape
     quarter = rows_hi // (size_y * size_z)
+    channels = lift_weight.shape[1]
+    lift_shape = (span, span // features * channels)
+    copy_rows = (
+        lax.broadcasted_iota(jnp.int32, (span, features), 0) % features
+        == lax.broadcasted_iota(jnp.int32, (span, features), 1)
+    )
+    copy_columns = (
+        lax.broadcasted_iota(jnp.int32, (channels, lift_shape[1]), 1) % channels
+        == lax.broadcasted_iota(jnp.int32, (channels, lift_shape[1]), 0)
+    )
+    lift = dot(jnp.where(copy_rows, 1.0, 0.0).astype(BF16), lift_weight[...])
+    lift = dot(lift.astype(BF16), jnp.where(copy_columns, 1.0, 0.0).astype(BF16))
+    on_block = (
+        lax.broadcasted_iota(jnp.int32, lift_shape, 0) // features
+        == lax.broadcasted_iota(jnp.int32, lift_shape, 1) // channels
+    )
+    lift = jnp.where(on_block, lift, 0.0).astype(BF16)
     rest = summed[...]
     lifted = 0.0
     for piece in range(3):
         cut = rest.astype(BF16)
         rest = rest - cut.astype(F32)
-        lifted = lifted + dot(cut, lift[...])
+        lifted = lifted + dot(cut, lift)
     inside_y = pl.ds(1, size_y)
     for block in range(size_x // quarter):
         store_leaf(
@@ -270,14 +336,15 @@
     def leaf_layer(source, layer, emit):
         def block(x, count_x, y, count_y):
             swept = convolve(source, layer, x, count_x, y, count_y)
-            occupied = jnp.concatenate(
+            mask = jnp.concatenate(
                 [
-                    occ0[pl.ds((x + step) // BRICK, 1), y : y + count_y]
-                    for step in range(count_x)
+                    occupied[(x + step_x) // BRICK, (y + step_y) // BRICK, 0:size_z]
+                    for step_x in range(count_x)
+                    for step_y in range(count_y)
                 ],
                 0,
             )
-            emit(x, count_x, y, count_y, swept * occupied.reshape(swept.shape))
+            emit(x, count_x, y, count_y, swept * mask)
 
         def inner(step, carry):
             block(1 + 2 * step, 2, 1, size_y - 2)
@@ -307,6 +374,19 @@
     leaf_layer(leaf_a, 0, keep_first)
     halo.start(1, leaf_b)
     leaf_layer(leaf_b, 1, keep_second)
+
+    def widen(mask, factor):
+        size = mask.shape[0] * factor
+        return jnp.stack(
+            [
+                jnp.stack([mask[x // factor, y // factor] for y in range(size)])
+                for x in range(size)
+            ]
+        )
+
+    occ1 = widen(occupied[:, :, 0:size_z], BRICK // 2)
+    occ2 = widen(occupied[:, :, pl.ds(0, size_z // 2, 2)], BRICK // 4)
+    occ3 = occupied[:, :, size_z : size_z + size_z // 2]
 
     def coarse_conv(level, kernel, occupied):
         count, depth = kernel.shape[0] - 2, kernel.shape[2]
@@ -317,15 +397,17 @@
             window = window.reshape(count * count * depth, window.shape[-1]).astype(BF16)
             term = dot(window, coarse_convs[level, step])
             total = term if total is None else total + term
-        return jnp.maximum(total, 0.0).reshape(occupied.shape) * occupied[...]
+        return jnp.maximum(total, 0.0).reshape(occupied.shape) * occupied
 
     def finish_down(stage, buffer, total, occupied):
         count = occupied.shape[0]
-        cells = jnp.maximum(total, 0.0).reshape(occupied.shape) * occupied[...]
+        cells = jnp.maximum(total, 0.0).reshape(occupied.shape) * occupied
         buffer[1 : count + 1, 1 : count + 1] = cells
         halo.start(stage, buffer)
         halo.wait_arrived(stage, buffer)
 
+    for copy in weights:
+        copy.wait()
     total = 0.0
     leaf = leaf_out[...]
     for part in range(4):
@@ -350,7 +432,9 @@
     level_two[:, :, deep : 2 * deep] = jnp.zeros_like(occ2)
     level_two[:, :, 0:deep] = coarse_conv(1, stacked_z(coarse_b[...]), occ2)
     finish_down(4, coarse_c, shrink(1, level_two, occ3.shape[2]), occ3)
-    top_out[...] = coarse_conv(2, stacked_z(coarse_c[...]), occ3)
+    top = coarse_conv(2, stacked_z(coarse_c[...]), occ3)
+    top_out[...] = top[:, :, 0 : top_out.shape[2]].astype(BF16)
+    lax.fori_loop(1, senders, owner_sent, 0)
 
     for stage, buffer in enumerate((leaf_a, leaf_b, coarse_a, coarse_b, coarse_c)):
         halo.wait_sent(stage, buffer)
@@ -368,28 +452,35 @@
     down_coarse,
     coarse_convs,
 ):
-    arrived = lax.all_to_all(records[0], ("gx", "gy"), split_axis=0, concat_axis=0, tiled=True)
-    slots = lax.all_to_all(slot_voxels[0], ("gx", "gy"), split_axis=0, concat_axis=0, tiled=True)
     bricks_x, bricks_y, bricks_z = brick_mask.shape
     size_x, size_y, size_z = BRICK * bricks_x, BRICK * bricks_y, BRICK * bricks_z // 2
     features, channels = lift_weight.shape
     wide = down_leaf.shape[-1]
     rows_hi = size_x * size_y * size_z // 4
     span = 8 * features
-    occ0 = spread(jnp.repeat(brick_mask, BRICK, 1), 1, BRICK // 2)
-    occ1 = spread(brick_mask, BRICK // 2, BRICK // 2)
-    occ2 = spread(brick_mask, BRICK // 4, BRICK // 4)
-    occ3 = spread(brick_mask, 1, 1, 4)
+    senders, slot_rows, width = records.shape[1:]
+    cap = slot_voxels.shape[-1]
+    fine = jnp.repeat(brick_mask, BRICK // 2, 2)
+    padding = ((0, 0), (0, 0), (0, size_z // 2 - bricks_z))
+    mask = jnp.concatenate([fine, jnp.pad(brick_mask, padding)], 2).astype(F32)
+    mask = jnp.broadcast_to(mask[..., None], mask.shape + (2 * channels,))
+    far = pl.BlockSpec(memory_space=pl.ANY)
     vmem = pl.BlockSpec(memory_space=pltpu.VMEM)
     leaf, top = pl.pallas_call(
         functools.partial(encoder, n_gx, n_gy),
         out_shape=(
             jax.ShapeDtypeStruct((size_x, size_y, size_z, 2 * channels), BF16),
-            jax.ShapeDtypeStruct(occ3.shape, F32),
+            jax.ShapeDtypeStruct((bricks_x, bricks_y, bricks_z, wide), BF16),
         ),
-        in_specs=[vmem] * 11,
+        in_specs=[far, vmem, vmem, vmem, vmem, far, far, vmem],
         out_specs=(vmem, vmem),
         scratch_shapes=[
+            pltpu.VMEM((senders, slot_rows, width), BF16),
+            pltpu.VMEM((senders, 1, cap), jnp.int32),
+            pltpu.VMEM((senders, 1, cap), jnp.int32),
+            pltpu.VMEM((2, 9, 4 * channels, 2 * channels), BF16),
+            pltpu.VMEM((2, 8, wide, wide), BF16),
+            pltpu.VMEM((3, 9, 3 * wide, wide), BF16),
             pltpu.VMEM((rows_hi, span), F32),
             pltpu.VMEM((size_x + 2, size_y + 2, size_z, 4 * channels), BF16),
             pltpu.VMEM((size_x + 2, size_y + 2, size_z, 4 * channels), BF16),
@@ -401,6 +492,9 @@
             pltpu.VMEM((size_x // 4, size_y // 4, size_z, wide), F32),
             pltpu.SemaphoreType.DMA((5, 8)),
             pltpu.SemaphoreType.DMA((5, 8)),
+            pltpu.SemaphoreType.DMA((2, senders)),
+            pltpu.SemaphoreType.DMA((2, senders)),
+            pltpu.SemaphoreType.DMA((3,)),
         ],
         compiler_params=pltpu.CompilerParams(
             collective_id=0, has_side_effects=True, vmem_limit_bytes=56 * 1024 * 1024
@@ -409,19 +503,16 @@
             flops=30_000_000_000, bytes_accessed=10_000_000, transcendentals=0
         ),
     )(
-        arrived,
-        slots,
-        lift_blocks(lift_weight, 8),
-        leaf_taps(leaf_convs),
+        records[0],
+        slot_voxels[0],
+        lift_weight,
+        leaf_convs.reshape(2, 9, 3, channels, channels),
         down_leaf.reshape(4, 2 * channels, wide),
         down_coarse.reshape(2, 8, wide, wide),
         coarse_convs.reshape(3, 9, 3 * wide, wide),
-        occ0,
-        occ1,
-        occ2,
-        occ3,
-    )
-    return leaf, top[:, :, :bricks_z].astype(BF16)
+        mask,
+    )
+    return leaf, top
 
 
 def solution(mesh):

time: 87.9 us -> 64 us (0.73)
  waiting for transfers between devices: 16 us -> 0 us
  Pallas kernels: 46 us -> 57.1 us
  starting transfers between devices: 10.1 us -> 0 us
  local copies, waits for them, and re-layouts: 11.3 us -> 5.24 us
  other arithmetic: 3.3 us -> 0.76 us
    all_to_all x2 -> x0, waiting for transfers between devices: 16 us -> none  [the longest x1 12.1 us: per_device(): lax.all_to_all(records[0], ('gx', 'gy'), split_axis=0, concat_axis=0, til...]
    pallas_call x1, Pallas kernels: 46 us -> 57.1 us  [per_device(): pl.pallas_call(functools.partial(encoder, n_gx, n_gy), out_shape=(jax.Sha...]
    all_to_all x2 -> x0, starting transfers between devices: 10.1 us -> none  [the longest x1 7.1 us: per_device(): lax.all_to_all(slot_voxels[0], ('gx', 'gy'), split_axis=0, concat_axis=0,...]
    broadcast_in_dim x13 -> x2, local copies, waits for them, and re-layouts: 3.46 us -> 1.45 us  [the longest x1 0.75 us: per_device(): fine = jnp.repeat(brick_mask, BRICK // 2, 2)]
    concatenate x1 -> x0, other arithmetic: 1.69 us -> none  [leaf_taps(): taps = jnp.concatenate([first, second], -1)]
    all_to_all x1 -> x0, local copies, waits for them, and re-layouts: 1.47 us -> none  [per_device(): lax.all_to_all(slot_voxels[0], ('gx', 'gy'), split_axis=0, concat_axis=0,...]
    slice x1 -> x0, local copies, waits for them, and re-layouts: 1.31 us -> none  [per_device(): return (leaf, top[:, :, :bricks_z].astype(BF16))]
    another operation x2 -> x0, local copies, waits for them, and re-layouts: 1.09 us -> none  [lift_blocks(): tiled = jnp.tile(lift_weight, (copies, copies))]
  transfers between devices with their start and end apart: 2 -> 0, of which waited for: 2 -> 0; matrix products, arithmetic and copies ran while one was open for 7% -> 0% of each run, Pallas kernels for 0% -> 0%
where the time goes in v2:
time: 64 us; the launch traced here: 63.7 us
  Pallas kernels  57.1 us (89%)
  local copies, waits for them, and re-layouts  5.24 us (8%)
  other arithmetic  0.76 us (1%)
  between operations  0.64 us (1%)
    pallas_call x1, Pallas kernels, per_device(): pl.pallas_call(functools.partial(encoder, n_gx, n_gy), out_shape=(jax.Sha...  57.1 us
    unnamed x2, local copies, waits for them, and re-layouts  3.7 us

profile of v2, /device:TPU:1, one launch (start us, length us, event | category | flops | bytes accessed | tf_op | source)
XLA Modules:
  0.0 63.7 jit_solution(17196049825833075429)
XLA Ops:
  0.6 0.8 %broadcast_in_dim.4 = s32[2,2,4,4]{3,2,1,0:T(4,128)S(1)} broadcast(s32[2,2,4]{2,1,0:T(2,128)} %param.10), dimensions={0,1,2} | broadcast | bytes 320 | tf_op jit(solution)/shard_map/broadcast_in_dim | solution.py:463
  1.4 0.1 concatenate.9
  1.5 0.8 %fusion = f32[2,2,24]{2,1,0:T(2,128)S(1)} fusion(s32[2,2,4]{2,1,0:T(2,128)} %param.10, s32[2,2,16]{2,1,0:T(2,128)S(1)} %concatenate.9), kind=kLoop, calls=%fused_computation.1 | loop fusion | flops 192 | bytes 704 | tf_op jit(solution)/shard_map/convert_element_type | solution.py:465
  2.2 0.7 %broadcast_in_dim.10.occupied = f32[2,2,24,128]{3,2,1,0:T(8,128)} broadcast(f32[2,2,24]{2,1,0:T(2,128)S(1)} %fusion), dimensions={0,1,2} | broadcast | bytes 49536 | tf_op jit(solution)/shard_map/broadcast_in_dim | solution.py:466
  2.9 57.1 %shard_map.95 = (bf16[16,16,16,128]{3,2,1,0:T(8,128)(2,1)}, bf16[2,2,4,128]{3,2,1,0:T(4,128)(2,1)}) custom-call(bf16[32,64,128]{2,1,0:T(8,128)(2,1)} %bitcast.8, s32[32,256]{1,0:T(8,128)} %bitcast.11, bf16[32,64]{1,0:T(8,128)(2,1)} %lift_weight.1, bf16[2,9,3,64,64]{4,3,2,1,0:T(8,128)(2,1)} %bitcast.7, bf16[4,128,128]{2,1,0:T(8,128)(2,1)} %bitcast.10, ...), custom_call_target="tpu_custom_call" | custom-call | flops 30000001024 | bytes 10000000 | tf_op jit(solution)/shard_map/pallas_call | solution.py:469
  60.0 2.4 %copy.12 = bf16[16,16,16,128]{3,2,1,0:T(8,128)(2,1)} copy(bf16[16,16,16,128]{3,2,1,0:T(8,128)(2,1)} %get-tuple-element.4) | data formatting | bytes 2097152
  62.5 1.3 %copy.13 = bf16[2,2,4,128]{3,2,1,0:T(4,128)(2,1)} copy(bf16[2,2,4,128]{3,2,1,0:T(4,128)(2,1)} %get-tuple-element.5) | data formatting | bytes 8192

commit v3 on v2

--- a/solution.py
+++ b/solution.py
@@ -15,6 +15,16 @@
 
 def dot(left, right):
     return jnp.dot(left, right, preferred_element_type=F32)
+
+
+def over(value, size):
+    if size & (size - 1):
+        return value // size
+    return lax.shift_right_logical(value, jnp.full_like(value, size.bit_length() - 1))
+
+
+def within(value, size):
+    return value % size if size & (size - 1) else value & (size - 1)
 
 
 def side_parts(count, here, other):
@@ -81,7 +91,7 @@
 
 def shift_rows(rows, period):
     count = rows.shape[0]
-    z = lax.broadcasted_iota(jnp.int32, rows.shape, 0) % period
+    z = within(lax.broadcasted_iota(jnp.int32, rows.shape, 0), period)
     before = jnp.where(z == 0, 0.0, pltpu.roll(rows, 1, 0))
     after = jnp.where(z == period - 1, 0.0, pltpu.roll(rows, count - 1, 0))
     return before, after
@@ -118,9 +128,10 @@
     down_leaf,
     down_coarse_far,
     coarse_convs_far,
-    occupied,
+    brick_mask,
     leaf_out,
     top_out,
+    occupied,
     arrived,
     slots_out,
     slots_in,
@@ -219,6 +230,17 @@
     for copy in weights:
         copy.start()
 
+    bricks_x, bricks_y, bricks_z = brick_mask.shape
+    mask_rows, fine_rows = occupied.shape[2], leaf_out.shape[2]
+    row = lax.broadcasted_iota(jnp.int32, (mask_rows, bricks_z), 0)
+    brick = jnp.where(row < fine_rows, over(row, BRICK // 2), row - fine_rows)
+    here = brick == lax.broadcasted_iota(jnp.int32, (mask_rows, bricks_z), 1)
+    for brick_x in range(bricks_x):
+        for brick_y in range(bricks_y):
+            line = brick_mask[brick_x, brick_y : brick_y + 1, :].astype(F32)
+            line = jnp.sum(jnp.where(here, line, 0.0), axis=1, keepdims=True)
+            occupied[brick_x, brick_y] = jnp.broadcast_to(line, occupied.shape[2:])
+
     for layer in range(2):
         for step in range(9):
             low, mid, high = (leaf_convs[layer, step, tap] for tap in range(3))
@@ -237,16 +259,14 @@
     order_from = lax.broadcasted_iota(jnp.int32, (cap, cap), 0)
     order_to = lax.broadcasted_iota(jnp.int32, (cap, cap), 1)
     order = jnp.where(
-        order_from == (order_to % slot_rows) * lanes + order_to // slot_rows, 1.0, 0.0
+        order_from == within(order_to, slot_rows) * lanes + over(order_to, slot_rows), 1.0, 0.0
     ).astype(BF16)
     pick_from = lax.broadcasted_iota(jnp.int32, (width, lanes * span), 0)
     pick_to = lax.broadcasted_iota(jnp.int32, (width, lanes * span), 1)
     pick = jnp.where(
-        pick_from == (pick_to // span) * features + pick_to % features, 1.0, 0.0
+        pick_from == over(pick_to, span) * features + within(pick_to, features), 1.0, 0.0
     ).astype(BF16)
-    column_group = (
-        lax.broadcasted_iota(jnp.int32, (cap, span), 1) // features
-    ).astype(F32)
+    column_group = over(lax.broadcasted_iota(jnp.int32, (cap, span), 1), features).astype(F32)
     row_index = lax.broadcasted_iota(jnp.int32, (rows_hi, cap), 0).astype(F32)
     summed[...] = jnp.zeros_like(summed)
 
@@ -255,11 +275,10 @@
         lax.fori_loop(jnp.where(step > 0, base, 1), base + 8, owner_arrived, 0)
         index = jnp.concatenate([slots_in[base + place] for place in range(8)], 0)
         wide_all = dot(arrived[pl.ds(base, 8)].reshape(8 * slot_rows, width), pick)
-        half = index // 2
-        high = half % rows_hi
-        low = (index // (2 * rows_hi)) * 2 + index % 2
-        high_row = 64.0 * dot((high // 64).astype(F32).astype(BF16), order) + dot(
-            (high % 64).astype(F32).astype(BF16), order
+        high = within(over(index, 2), rows_hi)
+        low = over(index, 2 * rows_hi) * 2 + within(index, 2)
+        high_row = 64.0 * dot(over(high, 64).astype(F32).astype(BF16), order) + dot(
+            within(high, 64).astype(F32).astype(BF16), order
         )
         low_column = lax.dot_general(
             order,
@@ -293,18 +312,18 @@
     channels = lift_weight.shape[1]
     lift_shape = (span, span // features * channels)
     copy_rows = (
-        lax.broadcasted_iota(jnp.int32, (span, features), 0) % features
+        within(lax.broadcasted_iota(jnp.int32, (span, features), 0), features)
         == lax.broadcasted_iota(jnp.int32, (span, features), 1)
     )
     copy_columns = (
-        lax.broadcasted_iota(jnp.int32, (channels, lift_shape[1]), 1) % channels
+        within(lax.broadcasted_iota(jnp.int32, (channels, lift_shape[1]), 1), channels)
         == lax.broadcasted_iota(jnp.int32, (channels, lift_shape[1]), 0)
     )
     lift = dot(jnp.where(copy_rows, 1.0, 0.0).astype(BF16), lift_weight[...])
     lift = dot(lift.astype(BF16), jnp.where(copy_columns, 1.0, 0.0).astype(BF16))
     on_block = (
-        lax.broadcasted_iota(jnp.int32, lift_shape, 0) // features
-        == lax.broadcasted_iota(jnp.int32, lift_shape, 1) // channels
+        over(lax.broadcasted_iota(jnp.int32, lift_shape, 0), features)
+        == over(lax.broadcasted_iota(jnp.int32, lift_shape, 1), channels)
     )
     lift = jnp.where(on_block, lift, 0.0).astype(BF16)
     rest = summed[...]
@@ -460,10 +479,6 @@
     span = 8 * features
     senders, slot_rows, width = records.shape[1:]
     cap = slot_voxels.shape[-1]
-    fine = jnp.repeat(brick_mask, BRICK // 2, 2)
-    padding = ((0, 0), (0, 0), (0, size_z // 2 - bricks_z))
-    mask = jnp.concatenate([fine, jnp.pad(brick_mask, padding)], 2).astype(F32)
-    mask = jnp.broadcast_to(mask[..., None], mask.shape + (2 * channels,))
     far = pl.BlockSpec(memory_space=pl.ANY)
     vmem = pl.BlockSpec(memory_space=pltpu.VMEM)
     leaf, top = pl.pallas_call(
@@ -475,6 +490,7 @@
         in_specs=[far, vmem, vmem, vmem, vmem, far, far, vmem],
         out_specs=(vmem, vmem),
         scratch_shapes=[
+            pltpu.VMEM((bricks_x, bricks_y, size_z + size_z // 2, 2 * channels), F32),
             pltpu.VMEM((senders, slot_rows, width), BF16),
             pltpu.VMEM((senders, 1, cap), jnp.int32),
             pltpu.VMEM((senders, 1, cap), jnp.int32),
@@ -510,7 +526,7 @@
         down_leaf.reshape(4, 2 * channels, wide),
         down_coarse.reshape(2, 8, wide, wide),
         coarse_convs.reshape(3, 9, 3 * wide, wide),
-        mask,
+        brick_mask,
     )
     return leaf, top
 

time: 64 us -> 61.6 us (0.963)
  local copies, waits for them, and re-layouts: 5.24 us -> 3.7 us
  other arithmetic: 0.76 us -> 0 us
    broadcast_in_dim x2 -> x0, local copies, waits for them, and re-layouts: 1.45 us -> none  [the longest x1 0.75 us: per_device(): fine = jnp.repeat(brick_mask, BRICK // 2, 2)]
    convert_element_type x1 -> x0, other arithmetic: 0.76 us -> none  [per_device(): mask = jnp.concatenate([fine, jnp.pad(brick_mask, padding)], 2).astype(F32)]
where the time goes in v3:
time: 61.6 us; the launch traced here: 61.4 us
  Pallas kernels  57.1 us (93%)
  local copies, waits for them, and re-layouts  3.7 us (6%)
  between operations  0.64 us (1%)
    pallas_call x1, Pallas kernels, per_device(): pl.pallas_call(functools.partial(encoder, n_gx, n_gy), out_shape=(jax.Sha...  57.1 us
    unnamed x2, local copies, waits for them, and re-layouts  3.7 us

profile of v3, /device:TPU:1, one launch (start us, length us, event | category | flops | bytes accessed | tf_op | source)
XLA Modules:
  0.0 61.4 jit_solution(8929070386899029914)
XLA Ops:
  0.6 57.1 %shard_map.95 = (bf16[16,16,16,128]{3,2,1,0:T(8,128)(2,1)}, bf16[2,2,4,128]{3,2,1,0:T(4,128)(2,1)}) custom-call(bf16[32,64,128]{2,1,0:T(8,128)(2,1)} %bitcast.8, s32[32,256]{1,0:T(8,128)} %bitcast.11, bf16[32,64]{1,0:T(8,128)(2,1)} %lift_weight.1, bf16[2,9,3,64,64]{4,3,2,1,0:T(8,128)(2,1)} %bitcast.7, bf16[4,128,128]{2,1,0:T(8,128)(2,1)} %bitcast.10, ...), custom_call_target="tpu_custom_call" | custom-call | flops 30000001024 | bytes 10000000 | tf_op jit(solution)/shard_map/pallas_call | solution.py:484
  57.7 2.4 %copy.12 = bf16[16,16,16,128]{3,2,1,0:T(8,128)(2,1)} copy(bf16[16,16,16,128]{3,2,1,0:T(8,128)(2,1)} %get-tuple-element.4) | data formatting | bytes 2097152
  60.1 1.3 %copy.13 = bf16[2,2,4,128]{3,2,1,0:T(4,128)(2,1)} copy(bf16[2,2,4,128]{3,2,1,0:T(4,128)(2,1)} %get-tuple-element.5) | data formatting | bytes 8192

commit v4 on v3

--- a/solution.py
+++ b/solution.py
@@ -345,12 +345,12 @@
     halo.start(0, leaf_a)
 
     def convolve(source, layer, x, count_x, y, count_y):
-        total = None
+        windows = []
         for step in range(9):
             window = source[pl.ds(x + step // 3, count_x), pl.ds(y + step % 3, count_y)]
-            term = dot(window.reshape(-1, window.shape[-1]), taps[layer, step])
-            total = term if total is None else total + term
-        return jnp.maximum(total, 0.0)
+            windows.append(window.reshape(-1, window.shape[-1]))
+        table = taps[layer].reshape(-1, taps.shape[-1])
+        return jnp.maximum(dot(jnp.concatenate(windows, -1), table), 0.0)
 
     def leaf_layer(source, layer, emit):
         def block(x, count_x, y, count_y):

time: 61.6 us -> 61.6 us (level)
  no operation moved by 1% of the time
where the time goes in v4:
time: 61.6 us; the launch traced here: 61.4 us
  Pallas kernels  57.1 us (93%)
  local copies, waits for them, and re-layouts  3.7 us (6%)
  between operations  0.64 us (1%)
    pallas_call x1, Pallas kernels, per_device(): pl.pallas_call(functools.partial(encoder, n_gx, n_gy), out_shape=(jax.Sha...  57.1 us
    unnamed x2, local copies, waits for them, and re-layouts  3.7 us

profile of v4, /device:TPU:1, one launch (start us, length us, event | category | flops | bytes accessed | tf_op | source)
XLA Modules:
  0.0 61.4 jit_solution(15360511291740590503)
XLA Ops:
  0.6 57.1 %shard_map.95 = (bf16[16,16,16,128]{3,2,1,0:T(8,128)(2,1)}, bf16[2,2,4,128]{3,2,1,0:T(4,128)(2,1)}) custom-call(bf16[32,64,128]{2,1,0:T(8,128)(2,1)} %bitcast.8, s32[32,256]{1,0:T(8,128)} %bitcast.11, bf16[32,64]{1,0:T(8,128)(2,1)} %lift_weight.1, bf16[2,9,3,64,64]{4,3,2,1,0:T(8,128)(2,1)} %bitcast.7, bf16[4,128,128]{2,1,0:T(8,128)(2,1)} %bitcast.10, ...), custom_call_target="tpu_custom_call" | custom-call | flops 30000001024 | bytes 10000000 | tf_op jit(solution)/shard_map/pallas_call | solution.py:484
  57.7 2.4 %copy.12 = bf16[16,16,16,128]{3,2,1,0:T(8,128)(2,1)} copy(bf16[16,16,16,128]{3,2,1,0:T(8,128)(2,1)} %get-tuple-element.4) | data formatting | bytes 2097152
  60.1 1.3 %copy.13 = bf16[2,2,4,128]{3,2,1,0:T(4,128)(2,1)} copy(bf16[2,2,4,128]{3,2,1,0:T(4,128)(2,1)} %get-tuple-element.5) | data formatting | bytes 8192
